TPU v7x, 32 devices: a whole 2x2x4 slice. The times are simulated.
32 devices in a mesh: seq: 4 (over z), wide: 8 (over y, x, core).
Axes of the slice: x: 2, y: 2, z: 4, core: 2. Of those that a mesh axis runs over, the one named last changes fastest.
Arguments:
- layer_input: bfloat16 [8192, 8192], P(('wide', 'seq')), may hold values from -6 to 6
- head_inputs: bfloat16 [8192, 8192], P(('wide', 'seq')), may hold values from -6 to 6
- output_grad: bfloat16 [8192, 8192], P(('wide', 'seq')), may hold values from -6 to 6
- step_raw: bfloat16 [8192, 128], P(('wide', 'seq'))
- state_write: bfloat16 [8192, 64], P(('wide', 'seq')), may hold values from -5 to 5
- state_read: bfloat16 [8192, 64], P(('wide', 'seq')), may hold values from -5 to 5
- decay_log: float32 [128], replicated
- step_bias: float32 [128], replicated, may hold values from -1 to 0.5
- skip_gain: float32 [128], replicated, may hold values from 0.5 to 1.5
Outputs:
- grad_x: bfloat16 [8192, 8192], P(('wide', 'seq'))
- weight_grad: float32 [8192, 256], P(('seq', 'wide'))
All inputs are finite; a program needn't handle non-finite values.
Results may differ from a plain program's by a relative error of at most 0.0029.
Values may be sent and summed in bfloat16 or wider, within the bound.
No kernel may reach another device: no remote copies, remote signals or barrier semaphores. Data moves between devices by JAX's collectives and lax.ppermute only.
A program may use at most 384 MiB of HBM per device.

v0:
```python
import functools
import math

import jax
import jax.numpy as jnp
from jax import lax
from jax.experimental import pallas as pl
from jax.experimental.pallas import tpu as pltpu
from jax.sharding import PartitionSpec as P

F32 = jnp.float32
BF16 = jnp.bfloat16
EXACT = lax.Precision.HIGHEST
VMEM_LIMIT = 64 * 1024 * 1024
TOP_POWER = 30.0
PRODUCT_BOUND = 30.0
CARRY_HEADS = 16
PAIR_HEADS = 8
META = 8
HALVES = 2
SHORT = pl.CostEstimate(flops=1000, bytes_accessed=1000, transcendentals=0)


def mul(a, b):
    return lax.dot_general(a, b, (((1,), (0,)), ((), ())), preferred_element_type=F32)


def mul_nt(a, b):
    return lax.dot_general(a, b, (((1,), (1,)), ((), ())), preferred_element_type=F32)


def mul_exact(a, b, dims=((1,), (0,))):
    return lax.dot_general(a, b, (dims, ((), ())), preferred_element_type=F32, precision=EXACT)


def halves(value):
    top = value.astype(BF16)
    return top, (value - top.astype(F32)).astype(BF16)


def power_for(bound):
    power = jnp.floor(TOP_POWER - jnp.log2(jnp.maximum(bound, 1e-37)))
    return jnp.clip(power, -100.0, 100.0)


def thirds(value):
    top, rest = value.astype(BF16), value
    rest = rest - top.astype(F32)
    middle = rest.astype(BF16)
    return top, middle, (rest - middle.astype(F32)).astype(BF16)


def encode(value):
    square = value * value
    fourth = square * square
    return jnp.where(value < 0, -fourth, fourth).astype(BF16)


def decode(coded):
    coded = coded.astype(F32)
    size = jnp.maximum(jnp.abs(coded), 1e-37)
    inverse = lax.rsqrt(size)
    return coded * inverse * lax.rsqrt(size * inverse)


def head_selector(first_head, heads, lanes, head_width):
    row = lax.broadcasted_iota(jnp.int32, (heads, lanes), 0)
    lane = lax.broadcasted_iota(jnp.int32, (heads, lanes), 1)
    return jnp.where(row == first_head + lane // head_width, 1.0, 0.0).astype(BF16)


def triangle(length, keep):
    row = lax.broadcasted_iota(jnp.int32, (length, length), 0)
    col = lax.broadcasted_iota(jnp.int32, (length, length), 1)
    return jnp.where(keep(row, col), 1.0, 0.0).astype(F32)


def summary_kernel(
    head_width,
    raw_ref,
    bias_ref,
    decay_ref,
    write_ref,
    read_ref,
    x_ref,
    dy_ref,
    message_ref,
    step_ref,
    cum_ref,
    weight_f,
    weight_b,
    facts,
):
    turn = pl.program_id(0)
    heads = raw_ref.shape[1]
    rows, lanes = x_ref.shape
    state = write_ref.shape[0]

    @pl.when(turn == 0)
    def _():
        step = jax.nn.softplus(raw_ref[...].astype(F32) + bias_ref[...])
        rate = -jnp.exp(decay_ref[...])
        cum = mul_exact(triangle(rows, lambda r, c: r >= c), step * rate)
        finish = cum[rows - 1 : rows, :]
        forward = step * jnp.exp(finish - cum)
        backward = jnp.exp(cum)
        power_f = power_for(PRODUCT_BOUND * jnp.sum(forward, axis=0, keepdims=True))
        power_b = power_for(PRODUCT_BOUND * jnp.sum(backward, axis=0, keepdims=True))
        step_ref[...] = step
        cum_ref[...] = cum
        parts = thirds(jnp.maximum(finish, -1e30))
        facts[...] = jnp.concatenate(
            [part.astype(F32) for part in parts]
            + [power_f, power_b, jnp.zeros((META - 5, heads), F32)],
            axis=0,
        ).astype(BF16)
        weight_f[...] = (forward * jnp.exp2(power_f)).T
        weight_b[...] = (backward * jnp.exp2(power_b)).T

    group = lanes // head_width
    pair_lanes = 2 * head_width
    width = message_ref.shape[2]
    near = pl.ds(turn * group, group)
    pick = head_selector(turn * group, heads, lanes, head_width)
    fact = mul(facts[...], pick).astype(BF16)
    lane = lax.broadcasted_iota(jnp.int32, (state, pair_lanes), 1)
    ahead = (x_ref, write_ref[...].astype(F32), weight_f[near, :], 0)
    behind = (dy_ref, read_ref[...].astype(F32), weight_b[near, :], state)
    for pair in range(group // 2):
        span = slice(pair * pair_lanes, (pair + 1) * pair_lanes)
        owner, offset = pair * pair_lanes // width, pair * pair_lanes % width
        here = slice(offset, offset + pair_lanes)
        for tokens_ref, rows_t, weights, start in (ahead, behind):
            scaled = []
            for head in (2 * pair, 2 * pair + 1):
                scaled += halves(rows_t * weights[head : head + 1, :])
            product = mul(jnp.concatenate(scaled, axis=0), tokens_ref[:, span])
            early = product[0:state] + product[state : 2 * state]
            late = product[2 * state : 3 * state] + product[3 * state :]
            total = jnp.where(lane < head_width, early, late)
            message_ref[owner, start : start + state, here] = encode(total)
        message_ref[owner, 2 * state :, here] = fact[:, span]


def scan_kernel(message_ref, *rest):
    answer_ref, powers = rest[-2:]
    blocks, double, lanes = message_ref.shape
    state = (double - META) // 2
    top = 2.0**TOP_POWER

    def one(block, start, power_row, side, running, bound):
        facts = message_ref[block, 2 * state : double, :].astype(F32)
        decay = jnp.exp(facts[0:1] + facts[1:2] + facts[2:3])
        back = jnp.exp2(-facts[power_row : power_row + 1])
        power = power_for(bound)
        powers[side, pl.ds(block, 1), :] = power
        answer_ref[block, start : start + state, :] = encode(running * jnp.exp2(power))
        own = decode(message_ref[block, start : start + state, :]) * back
        return running * decay + own, bound * decay + top * back

    def both(block, carry):
        ahead, ahead_bound, behind, behind_bound = carry
        return one(block, 0, 3, 0, ahead, ahead_bound) + one(
            blocks - 1 - block, state, 4, 1, behind, behind_bound
        )

    zero, none = jnp.zeros((state, lanes), F32), jnp.zeros((1, lanes), F32)
    lax.fori_loop(0, blocks, both, (zero, none, zero, none), unroll=4)
    row = lax.broadcasted_iota(jnp.int32, (blocks, META, lanes), 1)
    ahead, behind = powers[0][:, None, :], powers[1][:, None, :]
    meta = jnp.where(row == 0, ahead, jnp.where(row == 1, behind, 0.0))
    answer_ref[:, 2 * state : double, :] = meta.astype(BF16)


def block_kernel(
    head_width,
    scale,
    first_head,
    waits,
    step_ref,
    cum_ref,
    write_ref,
    read_ref,
    x_ref,
    dy_ref,
    *rest,
):
    inner_ref, own_ref, within_ref, maps_ref = rest[waits : waits + 4]
    read_write, source, cum_rows, pair_sum, out_flow = rest[waits + 4 :]
    turn = pl.program_id(0)
    rows, lanes = x_ref.shape
    half = rows // 2
    heads = step_ref.shape[1]
    group = lanes // head_width

    @pl.when(turn == 0)
    def _():
        read_write[...] = scale * lax.dot_general(
            write_ref[...], read_ref[...], (((0,), (0,)), ((), ())), preferred_element_type=F32
        )
        source[...] = jnp.log(step_ref[...]) - cum_ref[...]
        cum_rows[...] = cum_ref[...].T
        pair_sum[...] = jnp.zeros_like(pair_sum)
        out_flow[...] = jnp.zeros_like(out_flow)
        own_ref[...] = jnp.zeros_like(own_ref)

    first = first_head + turn * group
    near = pltpu.roll(source[...], lax.rem(heads - first, heads), axis=1)
    near_cum = cum_rows[pl.ds(first, group), :]
    row = lax.broadcasted_iota(jnp.int32, (half, half), 0)
    col = lax.broadcasted_iota(jnp.int32, (half, half), 1)
    ahead = col >= row
    lane = lax.broadcasted_iota(jnp.int32, (half, 2 * head_width), 1)
    first_half = lane < head_width
    head_lane = lax.broadcasted_iota(jnp.int32, (half, heads), 1)
    flow_aa = read_write[0:half, 0:half]
    flow_ab = read_write[0:half, half:rows]
    flow_bb = read_write[half:rows, half:rows]
    sum_aa = jnp.zeros((half, half), F32)
    sum_ab = jnp.zeros((half, half), F32)
    sum_bb = jnp.zeros((half, half), F32)
    own_a = jnp.zeros((half, heads), F32)
    own_b = jnp.zeros((half, heads), F32)
    zero = jnp.zeros((half, 2 * head_width), BF16)
    flows = []
    for pair in range(group // 2):
        span = slice(pair * 2 * head_width, (pair + 1) * 2 * head_width)
        x_a, x_b = x_ref[0:half, span], x_ref[half:rows, span]
        dy_a, dy_b = dy_ref[0:half, span], dy_ref[half:rows, span]
        early_a, late_a = jnp.where(first_half, dy_a, zero), jnp.where(first_half, zero, dy_a)
        early_b, late_b = jnp.where(first_half, dy_b, zero), jnp.where(first_half, zero, dy_b)
        stack = jnp.concatenate([early_a, early_b, late_a, late_b], axis=0)
        stack_b = jnp.concatenate([early_b, late_b], axis=0)
        grad_a = mul_nt(x_a, stack)
        grad_b = mul_nt(x_b, stack_b)
        masks_a, masks_b = [], []
        for side in range(2):
            place = pair * 2 + side
            head = first + place
            from_a = near[0:half, place : place + 1]
            from_b = near[half:rows, place : place + 1]
            to_a = near_cum[place : place + 1, 0:half]
            to_b = near_cum[place : place + 1, half:rows]
            fade_aa = jnp.exp(jnp.where(ahead, to_a + from_a, -1e30))
            fade_ab = jnp.exp(to_b + from_a)
            fade_bb = jnp.exp(jnp.where(ahead, to_b + from_b, -1e30))
            weigh_aa = fade_aa * grad_a[:, side * rows : side * rows + half]
            weigh_ab = fade_ab * grad_a[:, side * rows + half : (side + 1) * rows]
            weigh_bb = fade_bb * grad_b[:, side * half : (side + 1) * half]
            sum_aa += weigh_aa
            sum_ab += weigh_ab
            sum_bb += weigh_bb
            masks_a += [(fade_aa * flow_aa).astype(BF16), (fade_ab * flow_ab).astype(BF16)]
            masks_b += [(fade_bb * flow_bb).astype(BF16)]
            pair_aa = weigh_aa * flow_aa
            pair_ab = weigh_ab * flow_ab
            pair_bb = weigh_bb * flow_bb
            flow_out = jnp.sum(pair_aa + pair_ab, axis=1, keepdims=True)
            own_a = jnp.where(head_lane == head, flow_out, own_a)
            flow_out = jnp.sum(pair_bb, axis=1, keepdims=True)
            own_b = jnp.where(head_lane == head, flow_out, own_b)
            flow_in = [
                jnp.sum(pair_aa, axis=0, keepdims=True),
                jnp.sum(pair_ab, axis=0, keepdims=True) + jnp.sum(pair_bb, axis=0, keepdims=True),
            ]
            flows.append(jnp.concatenate(flow_in, axis=1))
        inner_ref[0:half, span] = mul(jnp.concatenate(masks_a, axis=1), stack).astype(BF16)
        inner_ref[half:rows, span] = mul(jnp.concatenate(masks_b, axis=1), stack_b).astype(BF16)
    out_flow[pl.ds(first, group), :] = jnp.concatenate(flows, axis=0)
    pair_sum[0:half, 0:half] += sum_aa
    pair_sum[0:half, half:rows] += sum_ab
    pair_sum[half:rows, half:rows] += sum_bb
    own_ref[0:half, :] += own_a
    own_ref[half:rows, :] += own_b

    @pl.when(turn == pl.num_programs(0) - 1)
    def _():
        net = own_ref[...] - out_flow[...].T
        within_ref[...] = mul_exact(triangle(rows, lambda r, c: r > c), net)
        weighted = scale * pair_sum[...]
        maps_ref[...] = jnp.concatenate(
            [
                mul_exact(weighted, read_ref[...].astype(F32), ((1,), (1,))),
                mul_exact(weighted, write_ref[...].astype(F32), ((0,), (1,))),
            ],
            axis=1,
        )


def carry_kernel(head_width, scale, first_head, parts, waits, first, last, *refs):
    refs = list(refs)
    take = lambda count: [refs.pop(0) for _ in range(count)]
    raw_ref, bias_ref, decay_ref, step_ref, cum_ref, write_ref, read_ref, skip_ref = take(8)
    x_ref, dy_ref, inner_ref, answer_ref = take(4)
    take(waits)
    if not first:
        early_sums, early_through, _ = take(3)
    if last:
        own_refs, within_refs, map_refs = take(parts), take(parts), take(parts)
        grad_ref, table_ref, sums, through, weight_e, weight_s, maps, picks = take(8)
    else:
        grad_ref, sums, through, weight_e, weight_s, maps, picks = take(7)
    turn = pl.program_id(0)
    rows, lanes = x_ref.shape
    heads = step_ref.shape[1]
    state = write_ref.shape[0]
    future, past = slice(0, heads), slice(heads, 2 * heads)
    write_sum = slice(2 * heads, 2 * heads + 2 * state)
    read_sum = slice(2 * heads + 2 * state, 2 * heads + 4 * state)

    @pl.when(turn == 0)
    def _():
        cum = cum_ref[...]
        finish = cum[rows - 1 : rows, :]
        weight_e[...] = step_ref[...] * jnp.exp(finish - cum) * scale
        weight_s[...] = jnp.exp(cum) * scale
        pick = head_selector(0, heads, lanes, head_width)
        picks[...] = jnp.concatenate([pick, pick], axis=0)
        write = write_ref[...].astype(F32).T.astype(BF16)
        read = read_ref[...].astype(F32).T.astype(BF16)
        maps[...] = jnp.concatenate([write, write, read, read], axis=1)
        if first:
            sums[...] = jnp.zeros_like(sums)
            through[...] = jnp.zeros_like(through)
        else:
            sums[...] = early_sums[...]
            through[...] = early_through[...]

    first_here = first_head + turn * (lanes // head_width)
    pick = picks[0:heads, :]

    def rolled(value, shift):
        return pltpu.roll(value, lax.rem(shift, heads), axis=1)

    def spread_of(weight):
        near = rolled(weight[...], heads - first_here)
        return mul(jnp.concatenate(halves(near), axis=1), picks[...])

    starts, ends = [], []
    for piece in range(answer_ref.shape[0]):
        back = jnp.exp2(-answer_ref[piece, 2 * state : 2 * state + META, :].astype(F32))
        starts.append(decode(answer_ref[piece, 0:state, :]) * back[0:1])
        ends.append(decode(answer_ref[piece, state : 2 * state, :]) * back[1:2])
    start = jnp.concatenate(starts, axis=1)
    end = jnp.concatenate(ends, axis=1)
    start_parts = jnp.concatenate(halves(start), axis=0)
    end_parts = jnp.concatenate(halves(end), axis=0)
    x = x_ref[...].astype(F32)
    dy = dy_ref[...].astype(F32)
    skip = jnp.concatenate(
        [part.astype(F32) for part in thirds(skip_ref[...])] + [jnp.zeros((5, heads), F32)], axis=0
    )
    skip = rolled(skip, heads - first_here).astype(BF16)
    skip = jnp.sum(mul(skip, pick), axis=0, keepdims=True)

    spread_e = spread_of(weight_e)
    carried = mul(maps[:, 0 : 2 * state], end_parts) * spread_e
    grad_ref[...] = (inner_ref[...].astype(F32) + skip * dy + carried).astype(BF16)
    top, low = halves(x * carried)
    sums[:, future] += rolled(mul_nt(top, pick) + mul_nt(low, pick), first_here)
    top, low = halves(x * spread_e)
    sums[:, write_sum] += mul_nt(top, end_parts) + mul_nt(low, end_parts)

    weighted = dy * spread_of(weight_s)
    top = (weighted * mul(maps[:, 2 * state : 4 * state], start_parts)).astype(BF16)
    sums[:, past] += rolled(mul_nt(top, pick), first_here)
    top, low = halves(weighted)
    sums[:, read_sum] += mul_nt(top, start_parts) + mul_nt(low, start_parts)

    both = jnp.broadcast_to(jnp.sum(start * end, axis=0, keepdims=True), (8, lanes))
    top, low = halves(both)
    through[...] += rolled(mul_nt(top, pick) + mul_nt(low, pick), first_here)

    if not last:
        return

    @pl.when(turn == pl.num_programs(0) - 1)
    def _():
        rate = -jnp.exp(decay_ref[...])
        step = step_ref[...]
        gate = jax.nn.sigmoid(raw_ref[...].astype(F32) + bias_ref[...])
        finish = cum_ref[rows - 1 : rows, :]
        to_come = sums[:, future]
        decay_grad = (
            sum(ref[...] for ref in within_refs)
            + mul_exact(triangle(rows, lambda r, c: r <= c), sums[:, past])
            + mul_exact(triangle(rows, lambda r, c: r > c), to_come)
            + jnp.exp(finish) * scale * through[0:1, :]
        )
        ratio = jnp.where(step > 1e-30, gate / jnp.maximum(step, 1e-30), 1.0)
        inner = sum(ref[...] for ref in own_refs) + to_come
        raw_grad = inner * ratio + rate * decay_grad * gate
        map_sum = sums[:, 2 * heads :] + 0.0
        write_all = map_sum[:, 0:state] + map_sum[:, state : 2 * state]
        read_all = map_sum[:, 2 * state : 3 * state] + map_sum[:, 3 * state :]
        map_grad = jnp.concatenate([write_all, read_all], axis=1)
        map_grad += sum(ref[...] for ref in map_refs)
        table_ref[...] = jnp.concatenate([raw_grad.T, map_grad.T], axis=0).astype(BF16)


def deal_kernel(place_ref, layer_ref, after_ref, *out_refs):
    width = out_refs[0].shape[2]
    for turn, out_ref in enumerate(out_refs):
        start = pl.multiple_of((place_ref[0] ^ turn) * width, width)
        out_ref[0, :, :] = layer_ref[:, pl.ds(start, width)]


def product_kernel(planes, place_ref, *refs):
    table_all, layer_all, sems = refs[-3:]
    wide = (len(refs) - 3 - planes) // 2
    table_refs, layer_refs = refs[:wide], refs[wide : 2 * wide]
    out_refs = refs[2 * wide : 2 * wide + planes]
    columns, rows = table_refs[0].shape
    copies = []
    for plane in range(planes):
        source = place_ref[1] ^ plane
        copies += [
            pltpu.make_async_copy(
                ref.at[source], layer_all.at[plane, pl.ds(turn * rows, rows)], sems.at[plane, turn]
            )
            for turn, ref in enumerate(layer_refs)
        ]
    for copy in copies:
        copy.start()
    for turn, ref in enumerate(table_refs):
        table_all[:, turn * rows : (turn + 1) * rows] = ref[...]
    for plane, out_ref in enumerate(out_refs):
        for turn in range(wide):
            copies[plane * wide + turn].wait()
        total = mul(table_all[...], layer_all[plane])
        most = jnp.max(jnp.abs(total), axis=0, keepdims=True)
        power = power_for(jnp.max(most, axis=1, keepdims=True))
        out_ref[0:columns, :] = encode(total * jnp.exp2(power))
        out_ref[columns:, :] = jnp.broadcast_to(power, out_ref[columns:, :].shape).astype(BF16)


def gather_kernel(factor, *refs):
    part_refs, out_ref = refs[:-1], refs[-1]
    columns = out_ref.shape[1]
    total = jnp.zeros((columns, out_ref.shape[0]), F32)
    for part_ref in part_refs:
        power = part_ref[columns:, :].astype(F32)[0:1]
        total += decode(part_ref[0:columns, :]) * jnp.exp2(-power)
    out_ref[...] = (total * factor).T


def swap(array, axis, turn):
    if turn == 0:
        return array
    count = lax.axis_size(axis)
    return lax.ppermute(array, axis, [(one, one ^ turn) for one in range(count)])


def whole(shape):
    return pl.BlockSpec(shape, lambda i: (0,) * len(shape))


def call(kernel, steps, in_specs, out, scratch, aliases=None):
    return pl.pallas_call(
        kernel,
        grid=(steps,),
        in_specs=in_specs,
        out_specs=[spec for spec, _, _ in out],
        out_shape=[jax.ShapeDtypeStruct(dims, dtype) for _, dims, dtype in out],
        scratch_shapes=[pltpu.VMEM(dims, dtype) for dims, dtype in scratch],
        compiler_params=pltpu.CompilerParams(vmem_limit_bytes=VMEM_LIMIT),
        cost_estimate=SHORT,
        input_output_aliases=aliases or {},
    )


def body(
    layer_input,
    head_inputs,
    output_grad,
    step_raw,
    state_write,
    state_read,
    decay_log,
    step_bias,
    skip_gain,
):
    rows, channels = head_inputs.shape
    heads = step_raw.shape[1]
    head_width = channels // heads
    state = state_write.shape[1]
    model = layer_input.shape[1]
    columns = heads + 2 * state
    axes = ("wide", "seq")
    wide, planes = lax.axis_size("wide"), lax.axis_size("seq")
    blocks = wide * planes
    own_model = model // blocks
    scale = float(rows * blocks * state) ** -0.5
    parts = HALVES if heads % (HALVES * blocks) == 0 else 1
    part_heads = heads // parts
    part_lanes = channels // parts
    owner_lanes = part_lanes // blocks
    piece_lanes = max(owner_lanes, 128)
    pieces = part_lanes // piece_lanes
    depth = 2 * state + META
    bias = step_bias[None, :]
    decay = decay_log[None, :]
    skip = skip_gain[None, :]
    write_t, read_t = state_write.T, state_read.T

    lanes = CARRY_HEADS * head_width
    steps = part_lanes // lanes
    here = lanes // piece_lanes

    def tokens(part, width):
        first = part * (part_lanes // width)
        return pl.BlockSpec((rows, width), lambda i: (0, first + i))

    message_spec = pl.BlockSpec((here, depth, piece_lanes), lambda i: (i, 0, 0))
    both_spec = pl.BlockSpec((here, depth, piece_lanes), lambda i: (i % steps, 0, i // steps))
    head_spec = whole((rows, heads))
    line_spec = whole((1, heads))
    map_spec = whole((state, rows))
    head_out = (head_spec, (rows, heads), F32)

    def exchange(array):
        return lax.all_to_all(array, axes, split_axis=0, concat_axis=0, tiled=True)

    def to_owner(array):
        if owner_lanes < piece_lanes:
            split = array.reshape(pieces, depth, piece_lanes // owner_lanes, owner_lanes)
            array = jnp.moveaxis(split, 2, 1).reshape(blocks, depth, owner_lanes)
        return exchange(array)

    def from_owner(array):
        array = exchange(array)
        if owner_lanes < piece_lanes:
            split = array.reshape(pieces, piece_lanes // owner_lanes, depth, owner_lanes)
            array = jnp.moveaxis(split, 1, 2).reshape(pieces, depth, piece_lanes)
        return array

    def scan(part, message, after):
        dims = (blocks, depth, owner_lanes)
        (answer,) = call(
            scan_kernel,
            1,
            [pl.BlockSpec(dims, lambda i: (0, 0, part))] + [anywhere] * len(after),
            [(whole(dims), dims, BF16)],
            [((2, blocks, owner_lanes), F32)],
        )(message, *after)
        return answer

    with jax.named_scope("summaries"):
        message, step, cum = call(
            functools.partial(summary_kernel, head_width),
            parts * steps,
            [head_spec, line_spec, line_spec, map_spec, map_spec, tokens(0, lanes), tokens(0, lanes)],
            [(both_spec, (pieces, depth, parts * piece_lanes), BF16), head_out, head_out],
            [((heads, rows), F32), ((heads, rows), F32), ((META, heads), BF16)],
        )(step_raw, bias, decay, write_t, read_t, head_inputs, output_grad)
    place = jnp.stack([lax.axis_index("wide"), lax.axis_index("seq")]).astype(jnp.int32)
    with jax.named_scope("layer"):
        if own_model % 128:
            cut = jnp.transpose(layer_input.reshape(rows, planes, wide, own_model), (2, 1, 0, 3))
            dealt = [
                lax.dynamic_index_in_dim(cut, place[0] ^ turn, 0, False) for turn in range(wide)
            ]
        else:
            dealt = pl.pallas_call(
                deal_kernel,
                grid_spec=pltpu.PrefetchScalarGridSpec(
                    num_scalar_prefetch=1,
                    grid=(planes,),
                    in_specs=[
                        pl.BlockSpec((rows, wide * own_model), lambda i, p: (0, i)),
                        pl.BlockSpec(memory_space=pl.ANY),
                    ],
                    out_specs=[pl.BlockSpec((1, rows, own_model), lambda i, p: (i, 0, 0))] * wide,
                ),
                out_shape=[jax.ShapeDtypeStruct((planes, rows, own_model), BF16)] * wide,
                compiler_params=pltpu.CompilerParams(vmem_limit_bytes=VMEM_LIMIT),
                cost_estimate=SHORT,
            )(place, layer_input, cum)
        layer_parts = [swap(one, "wide", turn) for turn, one in enumerate(dealt)]

    anywhere = pl.BlockSpec(memory_space=pltpu.HBM)

    def own_block(part, after):
        width = PAIR_HEADS * head_width
        here_spec = pl.BlockSpec((rows, width), lambda i: (0, i))
        return call(
            functools.partial(block_kernel, head_width, scale, part * part_heads, len(after)),
            part_lanes // width,
            [head_spec, head_spec, map_spec, map_spec, tokens(part, width), tokens(part, width)]
            + [anywhere] * len(after),
            [
                (here_spec, (rows, part_lanes), BF16),
                head_out,
                head_out,
                (whole((rows, 2 * state)), (rows, 2 * state), F32),
            ],
            [
                ((rows, rows), F32),
                ((rows, heads), F32),
                ((heads, rows), F32),
                ((rows, rows), F32),
                ((heads, rows), F32),
            ],
        )(step, cum, write_t, read_t, head_inputs, output_grad, *after)

    firsts = [turn for turn in (2, 4, 3, 5) if turn < wide]
    middle = [turn for turn in (6,) if turn < wide]
    with jax.named_scope("own_block"):
        own_parts = [own_block(0, dealt[:1])]
        if parts > 1:
            own_parts.append(own_block(1, [own_parts[0][1], layer_parts[1]]))
    with jax.named_scope("scan"):
        arrived = to_owner(message)
        returned, before = [], own_parts[-1][1]
        for part in range(parts):
            after = [layer_parts[turn] for turn in (firsts, middle)[part]]
            before = scan(part, arrived, [before] + after)
            returned.append(from_owner(before))

    sums_out = (whole((rows, 2 * heads + 4 * state)), (rows, 2 * heads + 4 * state), F32)
    through_out = (whole((8, heads)), (8, heads), F32)
    early = ()
    with jax.named_scope("carried"):
        for part in range(parts):
            first, last = part == 0, part == parts - 1
            in_specs = [head_spec, line_spec, line_spec, head_spec, head_spec, map_spec, map_spec]
            in_specs += [line_spec, tokens(part, lanes), tokens(part, lanes)]
            in_specs += [pl.BlockSpec((rows, lanes), lambda i: (0, i)), message_spec]
            operands = [step_raw, bias, decay, step, cum, write_t, read_t, skip]
            operands += [head_inputs, output_grad, own_parts[part][0], returned[part]]
            after = layer_parts[7:] if last else []
            operands += after
            in_specs += [anywhere] * len(after)
            aliases = {}
            if not first:
                in_specs += [sums_out[0], through_out[0], pl.BlockSpec(memory_space=pl.ANY)]
                operands += [early[1], early[2], early[0]]
                aliases = {len(operands) - 1: 0}
            scratch = [((rows, heads), F32)] * 2 + [((rows, 4 * state), BF16)]
            scratch += [((2 * heads, lanes), BF16)]
            out = [(tokens(part, lanes), (rows, channels), BF16)]
            if last:
                for which in (1, 2, 3):
                    operands += [one[which] for one in own_parts]
                    in_specs += [whole(one[which].shape) for one in own_parts]
                out += [(whole((columns, rows)), (columns, rows), BF16)]
                scratch = [sums_out[1:], through_out[1:]] + scratch
            else:
                out += [sums_out, through_out]
            early = call(
                functools.partial(
                    carry_kernel, head_width, scale, part * part_heads, parts, len(after), first, last
                ),
                steps,
                in_specs,
                out,
                scratch,
                aliases,
            )(*operands)
    grad_x, table = early

    with jax.named_scope("projection"):
        tables = [swap(table, "wide", turn) for turn in range(wide)]
        coded = (columns + META, own_model)
        products = pl.pallas_call(
            functools.partial(product_kernel, planes),
            in_specs=[pl.BlockSpec(memory_space=pltpu.SMEM)]
            + [pl.BlockSpec(memory_space=pltpu.VMEM)] * wide
            + [anywhere] * wide,
            out_specs=[pl.BlockSpec(memory_space=pltpu.VMEM)] * planes,
            out_shape=[jax.ShapeDtypeStruct(coded, BF16)] * planes,
            scratch_shapes=[
                pltpu.VMEM((columns, wide * rows), BF16),
                pltpu.VMEM((planes, wide * rows, own_model), BF16),
                pltpu.SemaphoreType.DMA((planes, wide)),
            ],
            compiler_params=pltpu.CompilerParams(vmem_limit_bytes=VMEM_LIMIT),
            cost_estimate=SHORT,
        )(place, *tables, *layer_parts)
        sums = [swap(one, "seq", turn) for turn, one in enumerate(products)]
        (weight_grad,) = call(
            functools.partial(gather_kernel, 1.0 / math.sqrt(rows * blocks)),
            1,
            [whole(coded)] * planes,
            [(whole((own_model, columns)), (own_model, columns), F32)],
            [],
        )(*sums)
    return grad_x, weight_grad


def solution(mesh):
    in_specs = (
        P(("wide", "seq"), None),
        P(("wide", "seq"), None),
        P(("wide", "seq"), None),
        P(("wide", "seq"), None),
        P(("wide", "seq"), None),
        P(("wide", "seq"), None),
        P(),
        P(),
        P(),
    )
    out_specs = (P(("wide", "seq"), None), P(("seq", "wide"), None))
    return jax.shard_map(body, mesh=mesh, in_specs=in_specs, out_specs=out_specs, check_vma=False)
```

profile of v0, /device:TPU:0, one launch (start us, length us, event | category | flops | bytes accessed | tf_op | source)
XLA Modules:
  0.0 195.3 jit_solution(6855383870851026734)
XLA Ops:
  0.6 11.0 %summaries.1 = (bf16[32,136,256]{2,1,0:T(8,128)(2,1)}, f32[256,128]{1,0:T(8,128)}, f32[256,128]{1,0:T(8,128)}) custom-call(bf16[256,128]{1,0:T(8,128)(2,1)} %refs_0_.3, f32[1,128]{1,0:T(1,128)} %bitcast.17, f32[1,128]{1,0:T(1,128)} %bitcast.20, bf16[64,256]{1,0:T(8,128)(2,1)} %bitcast.7, bf16[64,256]{1,0:T(8,128)(2,1)} %bitcast.12, ...), custom_call_target="tpu_custom_call" | custom-call | flops 1000 | bytes 1000 | tf_op jit(solution)/shard_map/summaries/pallas_call | solution.py:549
  11.6 7.4 %all-to-all-start = ((bf16[32,136,256]{2,1,0:T(8,128)(2,1)}), bf16[32,136,256]{2,1,0:T(8,128)(2,1)}, u32[]{:S(2)}, u32[]{:S(2)}) async-start(bf16[32,136,256]{2,1,0:T(8,128)(2,1)} %get-tuple-element.36), calls=%async_computation | async-start | bytes 4456448 | tf_op jit(solution)/shard_map/scan/all_to_all | solution.py:522
  19.0 0.7 pad_add_fusion.place_ref
  19.7 5.5 %layer.1 = (bf16[4,256,256]{2,1,0:T(8,128)(2,1)}, bf16[4,256,256]{2,1,0:T(8,128)(2,1)}, bf16[4,256,256]{2,1,0:T(8,128)(2,1)}, bf16[4,256,256]{2,1,0:T(8,128)(2,1...) custom-call(s32[2]{0:T(128)} %pad_add_fusion.place_ref, ...), custom_call_target="tpu_custom_call" | custom-call | flops 1000 | bytes 1000 | tf_op jit(solution)/shard_map/layer/pallas_call | solution.py:564
  25.2 0.3 collective-permute-start
  25.5 1.7 collective-permute-start.1
  27.1 1.5 collective-permute-start.2
  28.6 0.0 collective-permute-start.3
  28.6 0.6 collective-permute-start.4
  29.2 16.3 %own_block.2 = (bf16[256,4096]{1,0:T(8,128)(2,1)}, f32[256,128]{1,0:T(8,128)}, f32[256,128]{1,0:T(8,128)}, f32[256,128]{1,0:T(8,128)}) custom-call(f32[256,128]{1,0:T(8,128)} %get-tuple-element.30.step_ref.refs_3_, f32[256,128]{1,0:T(8,128)} %get-tuple-element.31.after_ref.cum_ref.refs_4_, bf16[64,256]{1,0:T(8,128)(2,1)} %bitcast.8, ...), custom_call_target="tpu_custom_call" | custom-call | flops 1000 | bytes 1000 | tf_op jit(solution)/shard_map/own_block/pallas_call | solution.py:586
  45.5 0.0 collective-permute-done.rest_1_.refs_9_
  45.5 16.7 %own_block.3 = (bf16[256,4096]{1,0:T(8,128)(2,1)}, f32[256,128]{1,0:T(8,128)}, f32[256,128]{1,0:T(8,128)}, f32[256,128]{1,0:T(8,128)}) custom-call(f32[256,128]{1,0:T(8,128)} %get-tuple-element.30.step_ref.refs_3_, f32[256,128]{1,0:T(8,128)} %get-tuple-element.31.after_ref.cum_ref.refs_4_, bf16[64,256]{1,0:T(8,128)(2,1)} %bitcast.9, ...), custom_call_target="tpu_custom_call" | custom-call | flops 1000 | bytes 1000 | tf_op jit(solution)/shard_map/own_block/pallas_call | solution.py:586
  62.2 0.0 collective-permute-done.1.rest_1_.refs_10_
  62.2 0.0 collective-permute-done.2.rest_2_.refs_12_
  62.2 4.9 %collective-permute-done.3.rest_3_.refs_11_ = bf16[4,256,256]{2,1,0:T(8,128)(2,1)} collective-permute-done((bf16[4,256,256]{2,1,0:T(8,128)(2,1)}, bf16[4,256,256]{2,1,0:T(8,128)(2,1)}, u32[]{:S(2)}, u32[]{:S(2)}) %collective-permute-start.3) | collective-permute-done | bytes 524320 | tf_op jit(solution)/shard_map/layer/ppermute | solution.py:451
  67.1 0.6 collective-permute-done.4.rest_4_.refs_13_
  67.7 1.8 all-to-all-done.message_ref
  69.4 3.9 %scan.2.rest_0_ = bf16[32,136,128]{2,1,0:T(8,128)(2,1)} custom-call(bf16[32,136,256]{2,1,0:T(8,128)(2,1)} %all-to-all-done.message_ref, f32[256,128]{1,0:T(8,128)} %get-tuple-element.37.rest_0_.refs_17_, bf16[4,256,256]{2,1,0:T(8,128)(2,1)} %collective-permute-done.1.rest_1_.refs_10_, bf16[4,256,256]{2,1,0:T(8,128)(2,1)} %collective-permute-done.2.rest_2_.refs_12_, ...), custom_call_target="tpu_custom_call" | custom-call | flops 1000 | bytes 1000 | tf_op jit(solution)/shard_map/scan/pallas_call | solution.py:539
  73.3 4.3 %all-to-all-start.2 = ((bf16[32,136,128]{2,1,0:T(8,128)(2,1)}), bf16[32,136,128]{2,1,0:T(8,128)(2,1)}, u32[]{:S(2)}, u32[]{:S(2)}) async-start(bf16[32,136,128]{2,1,0:T(8,128)(2,1)} %scan.2.rest_0_), calls=%async_computation.2 | async-start | bytes 2228224 | tf_op jit(solution)/shard_map/scan/all_to_all | solution.py:522
  77.7 2.7 %collective-permute-start.5 = (bf16[4,256,256]{2,1,0:T(8,128)(2,1)S(1)}, bf16[4,256,256]{2,1,0:T(8,128)(2,1)}, u32[]{:S(2)}, u32[]{:S(2)}) collective-permute-start(bf16[4,256,256]{2,1,0:T(8,128)(2,1)S(1)} %copy-done), channel_id=1, source_target_pairs={{0,6},{1,7},{2,4},{3,5},{4,2},{5,3},{6,0},{7,1},{8,14},{9,15},{10,... | collective-permute-start | bytes 1572872 | tf_op jit(solution)/shard_map/layer/ppermute | solution.py:451
  80.3 25.0 %collective-permute-done.5.rest_1_.refs_14_ = bf16[4,256,256]{2,1,0:T(8,128)(2,1)} collective-permute-done((bf16[4,256,256]{2,1,0:T(8,128)(2,1)S(1)}, bf16[4,256,256]{2,1,0:T(8,128)(2,1)}, u32[]{:S(2)}, u32[]{:S(2)}) %collective-permute-start.5) | collective-permute-done | bytes 524320 | tf_op jit(solution)/shard_map/layer/ppermute | solution.py:451
  105.3 3.9 %scan.3 = bf16[32,136,128]{2,1,0:T(8,128)(2,1)} custom-call(bf16[32,136,256]{2,1,0:T(8,128)(2,1)} %all-to-all-done.message_ref, bf16[32,136,128]{2,1,0:T(8,128)(2,1)} %scan.2.rest_0_, bf16[4,256,256]{2,1,0:T(8,128)(2,1)} %collective-permute-done.5.rest_1_.refs_14_), custom_call_target="tpu_custom_call" | custom-call | flops 1000 | bytes 1000 | tf_op jit(solution)/shard_map/scan/pallas_call | solution.py:539
  109.3 0.0 all-to-all-done.2.refs_11_
  109.3 5.0 %all-to-all-start.1 = ((bf16[32,136,128]{2,1,0:T(8,128)(2,1)}), bf16[32,136,128]{2,1,0:T(8,128)(2,1)}, u32[]{:S(2)}, u32[]{:S(2)}) async-start(bf16[32,136,128]{2,1,0:T(8,128)(2,1)} %scan.3), calls=%async_computation.1 | async-start | bytes 2228224 | tf_op jit(solution)/shard_map/scan/all_to_all | solution.py:522
  114.2 2.3 %collective-permute-start.6 = (bf16[4,256,256]{2,1,0:T(8,128)(2,1)}, bf16[4,256,256]{2,1,0:T(8,128)(2,1)}, u32[]{:S(2)}, u32[]{:S(2)}) collective-permute-start(bf16[4,256,256]{2,1,0:T(8,128)(2,1)} %get-tuple-element.43), channel_id=1, source_target_pairs={{0,7},{1,6},{2,5},{3,4},{4,3},{5,2},{6,1},{7,0},{8,15},{9,14},{10,... | collective-permute-start | bytes 1572872 | tf_op jit(solution)/shard_map/layer/ppermute | solution.py:451
  116.5 12.0 %carried.2 = (bf16[256,8192]{1,0:T(8,128)(2,1)}, f32[256,512]{1,0:T(8,128)}, f32[8,128]{1,0:T(8,128)}) custom-call(bf16[256,128]{1,0:T(8,128)(2,1)} %refs_0_.3, f32[1,128]{1,0:T(1,128)} %bitcast.18, f32[1,128]{1,0:T(1,128)} %bitcast.21, f32[256,128]{1,0:T(8,128)} %get-tuple-element.30.step_ref.refs_3_, ...), custom_call_target="tpu_custom_call" | custom-call | flops 1000 | bytes 1000 | tf_op jit(solution)/shard_map/carried/pallas_call | solution.py:650
  128.5 12.7 %collective-permute-done.6.refs_12_.refs_15_ = bf16[4,256,256]{2,1,0:T(8,128)(2,1)} collective-permute-done((bf16[4,256,256]{2,1,0:T(8,128)(2,1)}, bf16[4,256,256]{2,1,0:T(8,128)(2,1)}, u32[]{:S(2)}, u32[]{:S(2)}) %collective-permute-start.6) | collective-permute-done | bytes 524320 | tf_op jit(solution)/shard_map/layer/ppermute | solution.py:451
  141.3 13.3 %carried.3 = (bf16[256,8192]{1,0:T(8,128)(2,1)}, bf16[256,256]{1,0:T(8,128)(2,1)}) custom-call(bf16[256,128]{1,0:T(8,128)(2,1)} %refs_0_.3, f32[1,128]{1,0:T(1,128)} %bitcast.19, f32[1,128]{1,0:T(1,128)} %bitcast.22, f32[256,128]{1,0:T(8,128)} %get-tuple-element.30.step_ref.refs_3_, ...), custom_call_target="tpu_custom_call", output_to_operand_aliasing={{0}: (15, {})} | custom-call | flops 1000 | bytes 1000 | tf_op jit(solution)/shard_map/carried/pallas_call | solution.py:650
  154.6 1.9 collective-permute-start.13
  156.5 1.5 collective-permute-start.12
  158.0 1.5 collective-permute-start.10
  159.5 1.4 collective-permute-start.9
  160.9 0.0 collective-permute-done.13.refs_7_
  160.9 1.0 collective-permute-start.8
  161.9 3.6 %collective-permute-done.12.refs_6_ = bf16[256,256]{1,0:T(8,128)(2,1)} collective-permute-done((bf16[256,256]{1,0:T(8,128)(2,1)}, bf16[256,256]{1,0:T(8,128)(2,1)}, u32[]{:S(2)}, u32[]{:S(2)}) %collective-permute-start.12) | collective-permute-done | bytes 131104 | tf_op jit(solution)/shard_map/projection/ppermute | solution.py:451
  165.5 0.0 collective-permute-start.7
  165.5 1.8 collective-permute-done.11.refs_5_
  167.3 2.8 %collective-permute-done.10.refs_4_ = bf16[256,256]{1,0:T(8,128)(2,1)} collective-permute-done((bf16[256,256]{1,0:T(8,128)(2,1)}, bf16[256,256]{1,0:T(8,128)(2,1)}, u32[]{:S(2)}, u32[]{:S(2)}) %collective-permute-start.10) | collective-permute-done | bytes 131104 | tf_op jit(solution)/shard_map/projection/ppermute | solution.py:451
  170.1 0.0 collective-permute-done.9.refs_3_
  170.1 0.0 collective-permute-done.8.refs_2_
  170.1 0.0 collective-permute-done.7.refs_1_
  170.1 7.0 %projection.2 = (bf16[264,256]{1,0:T(8,128)(2,1)}, bf16[264,256]{1,0:T(8,128)(2,1)}, bf16[264,256]{1,0:T(8,128)(2,1)}, bf16[264,256]{1,0:T(8,128)(2,1)}) custom-call(s32[2]{0:T(128)} %pad_add_fusion.place_ref, bf16[256,256]{1,0:T(8,128)(2,1)} %get-tuple-element.53.refs_0_, bf16[256,256]{1,0:T(8,128)(2,1)} %collective-permute-done.7.refs_1_, ...), custom_call_target="tpu_custom_call" | custom-call | flops 1000 | bytes 1000 | tf_op jit(solution)/shard_map/projection/pallas_call | solution.py:665
  177.2 2.4 %collective-permute-start.14 = (bf16[264,256]{1,0:T(8,128)(2,1)}, bf16[264,256]{1,0:T(8,128)(2,1)}, u32[]{:S(2)}, u32[]{:S(2)}) collective-permute-start(bf16[264,256]{1,0:T(8,128)(2,1)} %get-tuple-element.55), channel_id=1, source_target_pairs={{0,8},{8,0},{16,24},{24,16},{1,9},{9,1},{17,25},{25,17},{2,10},{10... | collective-permute-start | bytes 405512 | tf_op jit(solution)/shard_map/projection/ppermute | solution.py:451
  179.6 1.7 collective-permute-start.15
  181.3 0.7 collective-permute-start.16
  182.0 3.5 %collective-permute-done.14.refs_1_ = bf16[264,256]{1,0:T(8,128)(2,1)} collective-permute-done((bf16[264,256]{1,0:T(8,128)(2,1)}, bf16[264,256]{1,0:T(8,128)(2,1)}, u32[]{:S(2)}, u32[]{:S(2)}) %collective-permute-start.14) | collective-permute-done | bytes 135200 | tf_op jit(solution)/shard_map/projection/ppermute | solution.py:451
  185.5 7.5 %collective-permute-done.15.refs_2_ = bf16[264,256]{1,0:T(8,128)(2,1)} collective-permute-done((bf16[264,256]{1,0:T(8,128)(2,1)}, bf16[264,256]{1,0:T(8,128)(2,1)}, u32[]{:S(2)}, u32[]{:S(2)}) %collective-permute-start.15) | collective-permute-done | bytes 135200 | tf_op jit(solution)/shard_map/projection/ppermute | solution.py:451
  193.1 2.2 %projection.3 = f32[256,256]{1,0:T(8,128)} custom-call(bf16[264,256]{1,0:T(8,128)(2,1)} %get-tuple-element.54.refs_0_, bf16[264,256]{1,0:T(8,128)(2,1)} %collective-permute-done.14.refs_1_, bf16[264,256]{1,0:T(8,128)(2,1)} %collective-permute-done.15.refs_2_, bf16[264,256]{1,0:T(8,128)(2,1)} %collective-permute-done.16.refs_3_), custom_call_target="tpu_custom_call" | custom-call | flops 1000 | bytes 1000 | tf_op jit(solution)/shard_map/projection/pallas_call | solution.py:681
  (5 shorter events, 0.0 us)
Async XLA Ops:
  11.6 57.9 %all-to-all-start = ((bf16[32,136,256]{2,1,0:T(8,128)(2,1)}), bf16[32,136,256]{2,1,0:T(8,128)(2,1)}, u32[]{:S(2)}, u32[]{:S(2)}) async-start(bf16[32,136,256]{2,1,0:T(8,128)(2,1)} %get-tuple-element.36), calls=%async_computation | async-start | bytes 4456448 | tf_op jit(solution)/shard_map/scan/all_to_all | solution.py:522
  25.2 20.3 %collective-permute-start = (bf16[4,256,256]{2,1,0:T(8,128)(2,1)}, bf16[4,256,256]{2,1,0:T(8,128)(2,1)}, u32[]{:S(2)}, u32[]{:S(2)}) collective-permute-start(bf16[4,256,256]{2,1,0:T(8,128)(2,1)} %get-tuple-element.34), channel_id=1, source_target_pairs={{0,1},{1,0},{2,3},{3,2},{4,5},{5,4},{6,7},{7,6},{8,9},{9,8},{10,11... | collective-permute-start | bytes 1572872 | tf_op jit(solution)/shard_map/layer/ppermute | solution.py:451
  25.5 36.7 %collective-permute-start.1 = (bf16[4,256,256]{2,1,0:T(8,128)(2,1)}, bf16[4,256,256]{2,1,0:T(8,128)(2,1)}, u32[]{:S(2)}, u32[]{:S(2)}) collective-permute-start(bf16[4,256,256]{2,1,0:T(8,128)(2,1)} %get-tuple-element.38), channel_id=1, source_target_pairs={{0,2},{1,3},{2,0},{3,1},{4,6},{5,7},{6,4},{7,5},{8,10},{9,11},{10,... | collective-permute-start | bytes 1572872 | tf_op jit(solution)/shard_map/layer/ppermute | solution.py:451
  27.1 35.1 %collective-permute-start.2 = (bf16[4,256,256]{2,1,0:T(8,128)(2,1)}, bf16[4,256,256]{2,1,0:T(8,128)(2,1)}, u32[]{:S(2)}, u32[]{:S(2)}) collective-permute-start(bf16[4,256,256]{2,1,0:T(8,128)(2,1)} %get-tuple-element.39), channel_id=1, source_target_pairs={{0,4},{1,5},{2,6},{3,7},{4,0},{5,1},{6,2},{7,3},{8,12},{9,13},{10,... | collective-permute-start | bytes 1572872 | tf_op jit(solution)/shard_map/layer/ppermute | solution.py:451
  28.6 38.5 %collective-permute-start.3 = (bf16[4,256,256]{2,1,0:T(8,128)(2,1)}, bf16[4,256,256]{2,1,0:T(8,128)(2,1)}, u32[]{:S(2)}, u32[]{:S(2)}) collective-permute-start(bf16[4,256,256]{2,1,0:T(8,128)(2,1)} %get-tuple-element.40), channel_id=1, source_target_pairs={{0,3},{1,2},{2,1},{3,0},{4,7},{5,6},{6,5},{7,4},{8,11},{9,10},{10,... | collective-permute-start | bytes 1572872 | tf_op jit(solution)/shard_map/layer/ppermute | solution.py:451
  28.6 39.1 %collective-permute-start.4 = (bf16[4,256,256]{2,1,0:T(8,128)(2,1)}, bf16[4,256,256]{2,1,0:T(8,128)(2,1)}, u32[]{:S(2)}, u32[]{:S(2)}) collective-permute-start(bf16[4,256,256]{2,1,0:T(8,128)(2,1)} %get-tuple-element.41), channel_id=1, source_target_pairs={{0,5},{1,4},{2,7},{3,6},{4,1},{5,0},{6,3},{7,2},{8,13},{9,12},{10,... | collective-permute-start | bytes 1572872 | tf_op jit(solution)/shard_map/layer/ppermute | solution.py:451
  73.3 4.4 %copy-start = (bf16[4,256,256]{2,1,0:T(8,128)(2,1)S(1)}, bf16[4,256,256]{2,1,0:T(8,128)(2,1)}, u32[]{:S(2)}) copy-start(bf16[4,256,256]{2,1,0:T(8,128)(2,1)} %get-tuple-element.42) | copy-start | bytes 1572868
  73.3 36.0 %all-to-all-start.2 = ((bf16[32,136,128]{2,1,0:T(8,128)(2,1)}), bf16[32,136,128]{2,1,0:T(8,128)(2,1)}, u32[]{:S(2)}, u32[]{:S(2)}) async-start(bf16[32,136,128]{2,1,0:T(8,128)(2,1)} %scan.2.rest_0_), calls=%async_computation.2 | async-start | bytes 2228224 | tf_op jit(solution)/shard_map/scan/all_to_all | solution.py:522
  77.7 27.6 %collective-permute-start.5 = (bf16[4,256,256]{2,1,0:T(8,128)(2,1)S(1)}, bf16[4,256,256]{2,1,0:T(8,128)(2,1)}, u32[]{:S(2)}, u32[]{:S(2)}) collective-permute-start(bf16[4,256,256]{2,1,0:T(8,128)(2,1)S(1)} %copy-done), channel_id=1, source_target_pairs={{0,6},{1,7},{2,4},{3,5},{4,2},{5,3},{6,0},{7,1},{8,14},{9,15},{10,... | collective-permute-start | bytes 1572872 | tf_op jit(solution)/shard_map/layer/ppermute | solution.py:451
  109.3 32.0 %all-to-all-start.1 = ((bf16[32,136,128]{2,1,0:T(8,128)(2,1)}), bf16[32,136,128]{2,1,0:T(8,128)(2,1)}, u32[]{:S(2)}, u32[]{:S(2)}) async-start(bf16[32,136,128]{2,1,0:T(8,128)(2,1)} %scan.3), calls=%async_computation.1 | async-start | bytes 2228224 | tf_op jit(solution)/shard_map/scan/all_to_all | solution.py:522
  114.2 27.0 %collective-permute-start.6 = (bf16[4,256,256]{2,1,0:T(8,128)(2,1)}, bf16[4,256,256]{2,1,0:T(8,128)(2,1)}, u32[]{:S(2)}, u32[]{:S(2)}) collective-permute-start(bf16[4,256,256]{2,1,0:T(8,128)(2,1)} %get-tuple-element.43), channel_id=1, source_target_pairs={{0,7},{1,6},{2,5},{3,4},{4,3},{5,2},{6,1},{7,0},{8,15},{9,14},{10,... | collective-permute-start | bytes 1572872 | tf_op jit(solution)/shard_map/layer/ppermute | solution.py:451
  154.6 6.3 %collective-permute-start.13 = (bf16[256,256]{1,0:T(8,128)(2,1)}, bf16[256,256]{1,0:T(8,128)(2,1)}, u32[]{:S(2)}, u32[]{:S(2)}) collective-permute-start(bf16[256,256]{1,0:T(8,128)(2,1)} %get-tuple-element.53.refs_0_), channel_id=1, source_target_pairs={{0,7},{1,6},{2,5},{3,4},{4,3},{5,2},{6,1},{7,0},{8,15},{9,14},{10,... | collective-permute-start | bytes 393224 | tf_op jit(solution)/shard_map/projection/ppermute | solution.py:451
  156.5 9.0 %collective-permute-start.12 = (bf16[256,256]{1,0:T(8,128)(2,1)}, bf16[256,256]{1,0:T(8,128)(2,1)}, u32[]{:S(2)}, u32[]{:S(2)}) collective-permute-start(bf16[256,256]{1,0:T(8,128)(2,1)} %get-tuple-element.53.refs_0_), channel_id=1, source_target_pairs={{0,6},{1,7},{2,4},{3,5},{4,2},{5,3},{6,0},{7,1},{8,14},{9,15},{10,... | collective-permute-start | bytes 393224 | tf_op jit(solution)/shard_map/projection/ppermute | solution.py:451
  158.0 9.3 %collective-permute-start.11 = (bf16[256,256]{1,0:T(8,128)(2,1)}, bf16[256,256]{1,0:T(8,128)(2,1)}, u32[]{:S(2)}, u32[]{:S(2)}) collective-permute-start(bf16[256,256]{1,0:T(8,128)(2,1)} %get-tuple-element.53.refs_0_), channel_id=1, source_target_pairs={{0,5},{1,4},{2,7},{3,6},{4,1},{5,0},{6,3},{7,2},{8,13},{9,12},{10,... | collective-permute-start | bytes 393224 | tf_op jit(solution)/shard_map/projection/ppermute | solution.py:451
  158.0 12.1 %collective-permute-start.10 = (bf16[256,256]{1,0:T(8,128)(2,1)}, bf16[256,256]{1,0:T(8,128)(2,1)}, u32[]{:S(2)}, u32[]{:S(2)}) collective-permute-start(bf16[256,256]{1,0:T(8,128)(2,1)} %get-tuple-element.53.refs_0_), channel_id=1, source_target_pairs={{0,4},{1,5},{2,6},{3,7},{4,0},{5,1},{6,2},{7,3},{8,12},{9,13},{10,... | collective-permute-start | bytes 393224 | tf_op jit(solution)/shard_map/projection/ppermute | solution.py:451
  159.5 10.6 %collective-permute-start.9 = (bf16[256,256]{1,0:T(8,128)(2,1)}, bf16[256,256]{1,0:T(8,128)(2,1)}, u32[]{:S(2)}, u32[]{:S(2)}) collective-permute-start(bf16[256,256]{1,0:T(8,128)(2,1)} %get-tuple-element.53.refs_0_), channel_id=1, source_target_pairs={{0,3},{1,2},{2,1},{3,0},{4,7},{5,6},{6,5},{7,4},{8,11},{9,10},{10,... | collective-permute-start | bytes 393224 | tf_op jit(solution)/shard_map/projection/ppermute | solution.py:451
  160.9 9.2 %collective-permute-start.8 = (bf16[256,256]{1,0:T(8,128)(2,1)}, bf16[256,256]{1,0:T(8,128)(2,1)}, u32[]{:S(2)}, u32[]{:S(2)}) collective-permute-start(bf16[256,256]{1,0:T(8,128)(2,1)} %get-tuple-element.53.refs_0_), channel_id=1, source_target_pairs={{0,2},{1,3},{2,0},{3,1},{4,6},{5,7},{6,4},{7,5},{8,10},{9,11},{10,... | collective-permute-start | bytes 393224 | tf_op jit(solution)/shard_map/projection/ppermute | solution.py:451
  165.5 4.6 %collective-permute-start.7 = (bf16[256,256]{1,0:T(8,128)(2,1)}, bf16[256,256]{1,0:T(8,128)(2,1)}, u32[]{:S(2)}, u32[]{:S(2)}) collective-permute-start(bf16[256,256]{1,0:T(8,128)(2,1)} %get-tuple-element.53.refs_0_), channel_id=1, source_target_pairs={{0,1},{1,0},{2,3},{3,2},{4,5},{5,4},{6,7},{7,6},{8,9},{9,8},{10,11... | collective-permute-start | bytes 393224 | tf_op jit(solution)/shard_map/projection/ppermute | solution.py:451
  177.2 8.4 %collective-permute-start.14 = (bf16[264,256]{1,0:T(8,128)(2,1)}, bf16[264,256]{1,0:T(8,128)(2,1)}, u32[]{:S(2)}, u32[]{:S(2)}) collective-permute-start(bf16[264,256]{1,0:T(8,128)(2,1)} %get-tuple-element.55), channel_id=1, source_target_pairs={{0,8},{8,0},{16,24},{24,16},{1,9},{9,1},{17,25},{25,17},{2,10},{10... | collective-permute-start | bytes 405512 | tf_op jit(solution)/shard_map/projection/ppermute | solution.py:451
  179.6 13.5 %collective-permute-start.15 = (bf16[264,256]{1,0:T(8,128)(2,1)}, bf16[264,256]{1,0:T(8,128)(2,1)}, u32[]{:S(2)}, u32[]{:S(2)}) collective-permute-start(bf16[264,256]{1,0:T(8,128)(2,1)} %get-tuple-element.56), channel_id=1, source_target_pairs={{0,16},{8,24},{16,0},{24,8},{1,17},{9,25},{17,1},{25,9},{2,18},{10... | collective-permute-start | bytes 405512 | tf_op jit(solution)/shard_map/projection/ppermute | solution.py:451
  181.3 11.8 %collective-permute-start.16 = (bf16[264,256]{1,0:T(8,128)(2,1)}, bf16[264,256]{1,0:T(8,128)(2,1)}, u32[]{:S(2)}, u32[]{:S(2)}) collective-permute-start(bf16[264,256]{1,0:T(8,128)(2,1)} %get-tuple-element.57), channel_id=1, source_target_pairs={{0,24},{8,16},{16,8},{24,0},{1,25},{9,17},{17,9},{25,1},{2,26},{10... | collective-permute-start | bytes 405512 | tf_op jit(solution)/shard_map/projection/ppermute | solution.py:451
where the time goes:
time: 196 us; the launch traced here: 195 us
  Pallas kernels  91.8 us (47%)
  waiting for transfers between devices  64.2 us (33%)
  starting transfers between devices  37.9 us (19%)
    ppermute x17, waiting for transfers between devices, swap(): lax.ppermute(array, axis, [(one, one ^ turn) for one in range(count)])  62.5 us
    pallas_call x2, Pallas kernels, own_block(): call(functools.partial(block_kernel, head_width, scale, part * part_heads...  32.9 us
    pallas_call x2, Pallas kernels, body(): call(functools.partial(carry_kernel, head_width, scale, part * part_heads...  25.3 us
    ppermute x17, starting transfers between devices, swap(): lax.ppermute(array, axis, [(one, one ^ turn) for one in range(count)])  21.1 us
    all_to_all x3, starting transfers between devices, exchange(): return lax.all_to_all(array, axes, split_axis=0, concat_axis=0, tiled=True)  16.7 us
    pallas_call x1, Pallas kernels, body(): call(functools.partial(summary_kernel, head_width), parts * steps, [head_...  11 us
    pallas_call x2, Pallas kernels, scan(): call(scan_kernel, 1, [pl.BlockSpec(dims, lambda i: (0, 0, part))] + [anyw...  7.81 us
    pallas_call x1, Pallas kernels, body(): pl.pallas_call(functools.partial(product_kernel, planes), in_specs=[pl.Bl...  7.03 us
  transfers between devices with their start and end apart: 20, of which 10 were waited for; matrix products, arithmetic and copies ran while one was open for 0% of the time, Pallas kernels for 28%

commit v1 on v0

--- a/solution.py
+++ b/solution.py
@@ -17,7 +17,6 @@
 CARRY_HEADS = 16
 PAIR_HEADS = 8
 META = 8
-HALVES = 2
 SHORT = pl.CostEstimate(flops=1000, bytes_accessed=1000, transcendentals=0)
 
 
@@ -287,23 +286,42 @@
         )
 
 
-def carry_kernel(head_width, scale, first_head, parts, waits, first, last, *refs):
-    refs = list(refs)
-    take = lambda count: [refs.pop(0) for _ in range(count)]
-    raw_ref, bias_ref, decay_ref, step_ref, cum_ref, write_ref, read_ref, skip_ref = take(8)
-    x_ref, dy_ref, inner_ref, answer_ref = take(4)
-    take(waits)
-    if not first:
-        early_sums, early_through, _ = take(3)
-    if last:
-        own_refs, within_refs, map_refs = take(parts), take(parts), take(parts)
-        grad_ref, table_ref, sums, through, weight_e, weight_s, maps, picks = take(8)
-    else:
-        grad_ref, sums, through, weight_e, weight_s, maps, picks = take(7)
+def spread_heads(weight, first_head, picks, group):
+    heads = weight.shape[1]
+    near = pltpu.roll(weight, lax.rem(heads - first_head, heads), axis=1)
+    top = near.astype(BF16).astype(F32)
+    low = pltpu.roll(near - top, group, axis=1)
+    lane = lax.broadcasted_iota(jnp.int32, near.shape, 1)
+    return mul(jnp.where(lane < group, top, low).astype(BF16), picks)
+
+
+def spread_picks(group, heads, lanes, head_width):
+    row = lax.broadcasted_iota(jnp.int32, (heads, lanes), 0)
+    lane = lax.broadcasted_iota(jnp.int32, (heads, lanes), 1)
+    match = jnp.where(row < group, row, row - group) == lane // head_width
+    return jnp.where(match, 1.0, 0.0).astype(BF16)
+
+
+def read_answer(answer_ref, state, power_row):
+    found = []
+    start = power_row * state
+    for piece in range(answer_ref.shape[0]):
+        facts = answer_ref[piece, 2 * state :, :].astype(F32)
+        back = jnp.exp2(-facts[power_row : power_row + 1])
+        found.append(decode(answer_ref[piece, start : start + state, :]) * back)
+    return jnp.concatenate(found, axis=1)
+
+
+def carry_kernel(head_width, scale, waits, *refs):
+    raw_ref, bias_ref, decay_ref, step_ref, cum_ref, write_ref, read_ref = refs[:7]
+    own_ref, within_ref, map_ref, x_ref, dy_ref, answer_ref = refs[7:13]
+    table_ref, sums, through, weight_e, weight_s, maps, picks = refs[13 + waits :]
     turn = pl.program_id(0)
     rows, lanes = x_ref.shape
     heads = step_ref.shape[1]
     state = write_ref.shape[0]
+    group = lanes // head_width
+    pair_lanes = 2 * head_width
     future, past = slice(0, heads), slice(heads, 2 * heads)
     write_sum = slice(2 * heads, 2 * heads + 2 * state)
     read_sum = slice(2 * heads + 2 * state, 2 * heads + 4 * state)
@@ -314,65 +332,58 @@
         finish = cum[rows - 1 : rows, :]
         weight_e[...] = step_ref[...] * jnp.exp(finish - cum) * scale
         weight_s[...] = jnp.exp(cum) * scale
-        pick = head_selector(0, heads, lanes, head_width)
-        picks[...] = jnp.concatenate([pick, pick], axis=0)
-        write = write_ref[...].astype(F32).T.astype(BF16)
-        read = read_ref[...].astype(F32).T.astype(BF16)
+        write, read = write_ref[...].astype(F32).T, read_ref[...].astype(F32).T
         maps[...] = jnp.concatenate([write, write, read, read], axis=1)
-        if first:
-            sums[...] = jnp.zeros_like(sums)
-            through[...] = jnp.zeros_like(through)
-        else:
-            sums[...] = early_sums[...]
-            through[...] = early_through[...]
-
-    first_here = first_head + turn * (lanes // head_width)
-    pick = picks[0:heads, :]
-
-    def rolled(value, shift):
-        return pltpu.roll(value, lax.rem(shift, heads), axis=1)
-
-    def spread_of(weight):
-        near = rolled(weight[...], heads - first_here)
-        return mul(jnp.concatenate(halves(near), axis=1), picks[...])
-
-    starts, ends = [], []
-    for piece in range(answer_ref.shape[0]):
-        back = jnp.exp2(-answer_ref[piece, 2 * state : 2 * state + META, :].astype(F32))
-        starts.append(decode(answer_ref[piece, 0:state, :]) * back[0:1])
-        ends.append(decode(answer_ref[piece, state : 2 * state, :]) * back[1:2])
-    start = jnp.concatenate(starts, axis=1)
-    end = jnp.concatenate(ends, axis=1)
-    start_parts = jnp.concatenate(halves(start), axis=0)
-    end_parts = jnp.concatenate(halves(end), axis=0)
-    x = x_ref[...].astype(F32)
-    dy = dy_ref[...].astype(F32)
-    skip = jnp.concatenate(
-        [part.astype(F32) for part in thirds(skip_ref[...])] + [jnp.zeros((5, heads), F32)], axis=0
-    )
-    skip = rolled(skip, heads - first_here).astype(BF16)
-    skip = jnp.sum(mul(skip, pick), axis=0, keepdims=True)
-
-    spread_e = spread_of(weight_e)
-    carried = mul(maps[:, 0 : 2 * state], end_parts) * spread_e
-    grad_ref[...] = (inner_ref[...].astype(F32) + skip * dy + carried).astype(BF16)
-    top, low = halves(x * carried)
-    sums[:, future] += rolled(mul_nt(top, pick) + mul_nt(low, pick), first_here)
-    top, low = halves(x * spread_e)
-    sums[:, write_sum] += mul_nt(top, end_parts) + mul_nt(low, end_parts)
-
-    weighted = dy * spread_of(weight_s)
-    top = (weighted * mul(maps[:, 2 * state : 4 * state], start_parts)).astype(BF16)
-    sums[:, past] += rolled(mul_nt(top, pick), first_here)
-    top, low = halves(weighted)
-    sums[:, read_sum] += mul_nt(top, start_parts) + mul_nt(low, start_parts)
+        picks[0:heads, :] = spread_picks(group, heads, lanes, head_width)
+        picks[heads:, :] = head_selector(0, heads, lanes, head_width)
+        sums[...] = jnp.zeros_like(sums)
+        through[...] = jnp.zeros_like(through)
+
+    first_here = turn * group
+    pick = picks[heads:, :]
+    early = lax.broadcasted_iota(jnp.int32, (state, pair_lanes), 1) < head_width
+    none = jnp.zeros((state, pair_lanes), BF16)
+    start = read_answer(answer_ref, state, 0)
+    end = read_answer(answer_ref, state, 1)
+
+    def products(tokens_ref, states, weight, map_columns):
+        spread = spread_heads(weight[...], first_here, picks[0:heads, :], group)
+        parts = halves(states)
+        total, mapped = 0.0, []
+        for pair in range(group // 2):
+            span = slice(pair * pair_lanes, (pair + 1) * pair_lanes)
+            blocks = [
+                jnp.concatenate(
+                    [jnp.where(early, part[:, span], none), jnp.where(early, none, part[:, span])],
+                    axis=0,
+                )
+                for part in parts
+            ]
+            twice = jnp.concatenate([tokens_ref[:, span], tokens_ref[:, span]], axis=1)
+            weighted = mul_nt(twice, jnp.concatenate(blocks, axis=1)) * spread[:, span]
+            total += weighted
+            mapped.append(weighted * map_columns)
+        return total, mapped
+
+    def summed(parts):
+        return mul_nt(jnp.concatenate(parts, axis=1), pick)
+
+    def placed(value):
+        return pltpu.roll(value, first_here, axis=1)
+
+    total, mapped = products(x_ref, end, weight_e, maps[:, 0 : 2 * state])
+    sums[:, write_sum] += total
+    mapped = [halves(one) for one in mapped]
+    to_come = summed([one[0] for one in mapped]) + summed([one[1] for one in mapped])
+    sums[:, future] += placed(to_come)
+
+    total, mapped = products(dy_ref, start, weight_s, maps[:, 2 * state : 4 * state])
+    sums[:, read_sum] += total
+    sums[:, past] += placed(summed([one.astype(BF16) for one in mapped]))
 
     both = jnp.broadcast_to(jnp.sum(start * end, axis=0, keepdims=True), (8, lanes))
     top, low = halves(both)
-    through[...] += rolled(mul_nt(top, pick) + mul_nt(low, pick), first_here)
-
-    if not last:
-        return
+    through[...] += placed(mul_nt(top, pick) + mul_nt(low, pick))
 
     @pl.when(turn == pl.num_programs(0) - 1)
     def _():
@@ -380,22 +391,47 @@
         step = step_ref[...]
         gate = jax.nn.sigmoid(raw_ref[...].astype(F32) + bias_ref[...])
         finish = cum_ref[rows - 1 : rows, :]
-        to_come = sums[:, future]
+        ahead = sums[:, future]
         decay_grad = (
-            sum(ref[...] for ref in within_refs)
+            within_ref[...]
             + mul_exact(triangle(rows, lambda r, c: r <= c), sums[:, past])
-            + mul_exact(triangle(rows, lambda r, c: r > c), to_come)
+            + mul_exact(triangle(rows, lambda r, c: r > c), ahead)
             + jnp.exp(finish) * scale * through[0:1, :]
         )
         ratio = jnp.where(step > 1e-30, gate / jnp.maximum(step, 1e-30), 1.0)
-        inner = sum(ref[...] for ref in own_refs) + to_come
-        raw_grad = inner * ratio + rate * decay_grad * gate
-        map_sum = sums[:, 2 * heads :] + 0.0
+        raw_grad = (own_ref[...] + ahead) * ratio + rate * decay_grad * gate
+        map_sum = sums[:, 2 * heads :]
         write_all = map_sum[:, 0:state] + map_sum[:, state : 2 * state]
         read_all = map_sum[:, 2 * state : 3 * state] + map_sum[:, 3 * state :]
-        map_grad = jnp.concatenate([write_all, read_all], axis=1)
-        map_grad += sum(ref[...] for ref in map_refs)
+        map_grad = jnp.concatenate([write_all, read_all], axis=1) + map_ref[...]
         table_ref[...] = jnp.concatenate([raw_grad.T, map_grad.T], axis=0).astype(BF16)
+
+
+def grad_kernel(head_width, scale, first_head, waits, *refs):
+    step_ref, cum_ref, write_ref, skip_ref, dy_ref, inner_ref, answer_ref = refs[:7]
+    grad_ref, weight_e, maps, picks = refs[7 + waits :]
+    turn = pl.program_id(0)
+    rows, lanes = dy_ref.shape
+    heads = step_ref.shape[1]
+    state = write_ref.shape[0]
+    group = lanes // head_width
+
+    @pl.when(turn == 0)
+    def _():
+        cum = cum_ref[...]
+        finish = cum[rows - 1 : rows, :]
+        weight_e[...] = step_ref[...] * jnp.exp(finish - cum) * scale
+        write = write_ref[...].astype(F32).T.astype(BF16)
+        maps[...] = jnp.concatenate([write, write], axis=1)
+        picks[...] = spread_picks(group, heads, lanes, head_width)
+
+    first_here = first_head + turn * group
+    end_parts = jnp.concatenate(halves(read_answer(answer_ref, state, 1)), axis=0)
+    skip = jnp.broadcast_to(skip_ref[...], (16, heads))
+    skip = spread_heads(skip, first_here, picks[...], group)[0:1]
+    carried = mul(maps[...], end_parts) * spread_heads(weight_e[...], first_here, picks[...], group)
+    inner = inner_ref[...].astype(F32)
+    grad_ref[...] = (inner + skip * dy_ref[...].astype(F32) + carried).astype(BF16)
 
 
 def deal_kernel(place_ref, layer_ref, after_ref, *out_refs):
@@ -405,37 +441,40 @@
         out_ref[0, :, :] = layer_ref[:, pl.ds(start, width)]
 
 
-def product_kernel(planes, place_ref, *refs):
+def product_kernel(planes, wide, place_ref, *refs):
+    table_refs, layer_refs = refs[:wide], refs[wide : 2 * wide]
+    out_refs = refs[-3 - planes : -3]
     table_all, layer_all, sems = refs[-3:]
-    wide = (len(refs) - 3 - planes) // 2
-    table_refs, layer_refs = refs[:wide], refs[wide : 2 * wide]
-    out_refs = refs[2 * wide : 2 * wide + planes]
     columns, rows = table_refs[0].shape
-    copies = []
+    loads = [
+        pltpu.make_async_copy(ref, table_all.at[turn], sems.at[planes, turn])
+        for turn, ref in enumerate(table_refs)
+    ]
     for plane in range(planes):
         source = place_ref[1] ^ plane
-        copies += [
+        loads += [
             pltpu.make_async_copy(
                 ref.at[source], layer_all.at[plane, pl.ds(turn * rows, rows)], sems.at[plane, turn]
             )
             for turn, ref in enumerate(layer_refs)
         ]
-    for copy in copies:
-        copy.start()
-    for turn, ref in enumerate(table_refs):
-        table_all[:, turn * rows : (turn + 1) * rows] = ref[...]
+    for load in loads:
+        load.start()
+    for load in loads[:wide]:
+        load.wait()
+    table = jnp.concatenate([table_all[turn] for turn in range(wide)], axis=1)
     for plane, out_ref in enumerate(out_refs):
-        for turn in range(wide):
-            copies[plane * wide + turn].wait()
-        total = mul(table_all[...], layer_all[plane])
+        for load in loads[(plane + 1) * wide : (plane + 2) * wide]:
+            load.wait()
+        total = mul(table, layer_all[plane])
         most = jnp.max(jnp.abs(total), axis=0, keepdims=True)
         power = power_for(jnp.max(most, axis=1, keepdims=True))
         out_ref[0:columns, :] = encode(total * jnp.exp2(power))
         out_ref[columns:, :] = jnp.broadcast_to(power, out_ref[columns:, :].shape).astype(BF16)
 
 
-def gather_kernel(factor, *refs):
-    part_refs, out_ref = refs[:-1], refs[-1]
+def gather_kernel(factor, planes, *refs):
+    part_refs, out_ref = refs[:planes], refs[-1]
     columns = out_ref.shape[1]
     total = jnp.zeros((columns, out_ref.shape[0]), F32)
     for part_ref in part_refs:
@@ -491,12 +530,9 @@
     blocks = wide * planes
     own_model = model // blocks
     scale = float(rows * blocks * state) ** -0.5
-    parts = HALVES if heads % (HALVES * blocks) == 0 else 1
-    part_heads = heads // parts
-    part_lanes = channels // parts
-    owner_lanes = part_lanes // blocks
+    owner_lanes = channels // blocks
     piece_lanes = max(owner_lanes, 128)
-    pieces = part_lanes // piece_lanes
+    pieces = channels // piece_lanes
     depth = 2 * state + META
     bias = step_bias[None, :]
     decay = decay_log[None, :]
@@ -504,15 +540,13 @@
     write_t, read_t = state_write.T, state_read.T
 
     lanes = CARRY_HEADS * head_width
-    steps = part_lanes // lanes
+    steps = channels // lanes
     here = lanes // piece_lanes
 
-    def tokens(part, width):
-        first = part * (part_lanes // width)
+    def tokens(width, first=0):
         return pl.BlockSpec((rows, width), lambda i: (0, first + i))
 
     message_spec = pl.BlockSpec((here, depth, piece_lanes), lambda i: (i, 0, 0))
-    both_spec = pl.BlockSpec((here, depth, piece_lanes), lambda i: (i % steps, 0, i // steps))
     head_spec = whole((rows, heads))
     line_spec = whole((1, heads))
     map_spec = whole((state, rows))
@@ -534,23 +568,12 @@
             array = jnp.moveaxis(split, 1, 2).reshape(pieces, depth, piece_lanes)
         return array
 
-    def scan(part, message, after):
-        dims = (blocks, depth, owner_lanes)
-        (answer,) = call(
-            scan_kernel,
-            1,
-            [pl.BlockSpec(dims, lambda i: (0, 0, part))] + [anywhere] * len(after),
-            [(whole(dims), dims, BF16)],
-            [((2, blocks, owner_lanes), F32)],
-        )(message, *after)
-        return answer
-
     with jax.named_scope("summaries"):
         message, step, cum = call(
             functools.partial(summary_kernel, head_width),
-            parts * steps,
-            [head_spec, line_spec, line_spec, map_spec, map_spec, tokens(0, lanes), tokens(0, lanes)],
-            [(both_spec, (pieces, depth, parts * piece_lanes), BF16), head_out, head_out],
+            steps,
+            [head_spec, line_spec, line_spec, map_spec, map_spec, tokens(lanes), tokens(lanes)],
+            [(message_spec, (pieces, depth, piece_lanes), BF16), head_out, head_out],
             [((heads, rows), F32), ((heads, rows), F32), ((META, heads), BF16)],
         )(step_raw, bias, decay, write_t, read_t, head_inputs, output_grad)
     place = jnp.stack([lax.axis_index("wide"), lax.axis_index("seq")]).astype(jnp.int32)
@@ -579,17 +602,16 @@
         layer_parts = [swap(one, "wide", turn) for turn, one in enumerate(dealt)]
 
     anywhere = pl.BlockSpec(memory_space=pltpu.HBM)
-
-    def own_block(part, after):
+    firsts = [turn for turn in (1, 2, 4, 3, 5) if turn < wide]
+    lasts = [layer_parts[turn] for turn in range(1, wide) if turn not in firsts]
+    with jax.named_scope("own_block"):
         width = PAIR_HEADS * head_width
-        here_spec = pl.BlockSpec((rows, width), lambda i: (0, i))
-        return call(
-            functools.partial(block_kernel, head_width, scale, part * part_heads, len(after)),
-            part_lanes // width,
-            [head_spec, head_spec, map_spec, map_spec, tokens(part, width), tokens(part, width)]
-            + [anywhere] * len(after),
+        inner, own, within, maps = call(
+            functools.partial(block_kernel, head_width, scale, 0, 1),
+            channels // width,
+            [head_spec, head_spec, map_spec, map_spec, tokens(width), tokens(width), anywhere],
             [
-                (here_spec, (rows, part_lanes), BF16),
+                (tokens(width), (rows, channels), BF16),
                 head_out,
                 head_out,
                 (whole((rows, 2 * state)), (rows, 2 * state), F32),
@@ -601,90 +623,85 @@
                 ((rows, rows), F32),
                 ((heads, rows), F32),
             ],
-        )(step, cum, write_t, read_t, head_inputs, output_grad, *after)
-
-    firsts = [turn for turn in (2, 4, 3, 5) if turn < wide]
-    middle = [turn for turn in (6,) if turn < wide]
-    with jax.named_scope("own_block"):
-        own_parts = [own_block(0, dealt[:1])]
-        if parts > 1:
-            own_parts.append(own_block(1, [own_parts[0][1], layer_parts[1]]))
+        )(step, cum, write_t, read_t, head_inputs, output_grad, dealt[0])
     with jax.named_scope("scan"):
-        arrived = to_owner(message)
-        returned, before = [], own_parts[-1][1]
-        for part in range(parts):
-            after = [layer_parts[turn] for turn in (firsts, middle)[part]]
-            before = scan(part, arrived, [before] + after)
-            returned.append(from_owner(before))
-
-    sums_out = (whole((rows, 2 * heads + 4 * state)), (rows, 2 * heads + 4 * state), F32)
-    through_out = (whole((8, heads)), (8, heads), F32)
-    early = ()
+        after = [own] + [layer_parts[turn] for turn in firsts]
+        dims = (blocks, depth, owner_lanes)
+        (answer,) = call(
+            scan_kernel,
+            1,
+            [whole(dims)] + [anywhere] * len(after),
+            [(whole(dims), dims, BF16)],
+            [((2, blocks, owner_lanes), F32)],
+        )(to_owner(message), *after)
+        returned = from_owner(answer)
+
     with jax.named_scope("carried"):
-        for part in range(parts):
-            first, last = part == 0, part == parts - 1
-            in_specs = [head_spec, line_spec, line_spec, head_spec, head_spec, map_spec, map_spec]
-            in_specs += [line_spec, tokens(part, lanes), tokens(part, lanes)]
-            in_specs += [pl.BlockSpec((rows, lanes), lambda i: (0, i)), message_spec]
-            operands = [step_raw, bias, decay, step, cum, write_t, read_t, skip]
-            operands += [head_inputs, output_grad, own_parts[part][0], returned[part]]
-            after = layer_parts[7:] if last else []
-            operands += after
-            in_specs += [anywhere] * len(after)
-            aliases = {}
-            if not first:
-                in_specs += [sums_out[0], through_out[0], pl.BlockSpec(memory_space=pl.ANY)]
-                operands += [early[1], early[2], early[0]]
-                aliases = {len(operands) - 1: 0}
-            scratch = [((rows, heads), F32)] * 2 + [((rows, 4 * state), BF16)]
-            scratch += [((2 * heads, lanes), BF16)]
-            out = [(tokens(part, lanes), (rows, channels), BF16)]
-            if last:
-                for which in (1, 2, 3):
-                    operands += [one[which] for one in own_parts]
-                    in_specs += [whole(one[which].shape) for one in own_parts]
-                out += [(whole((columns, rows)), (columns, rows), BF16)]
-                scratch = [sums_out[1:], through_out[1:]] + scratch
-            else:
-                out += [sums_out, through_out]
-            early = call(
-                functools.partial(
-                    carry_kernel, head_width, scale, part * part_heads, parts, len(after), first, last
-                ),
-                steps,
-                in_specs,
-                out,
-                scratch,
-                aliases,
-            )(*operands)
-    grad_x, table = early
+        (table,) = call(
+            functools.partial(carry_kernel, head_width, scale, len(lasts)),
+            steps,
+            [head_spec, line_spec, line_spec, head_spec, head_spec, map_spec, map_spec]
+            + [head_spec, head_spec, whole((rows, 2 * state))]
+            + [tokens(lanes), tokens(lanes), message_spec]
+            + [anywhere] * len(lasts),
+            [(whole((columns, rows)), (columns, rows), BF16)],
+            [
+                ((rows, 2 * heads + 4 * state), F32),
+                ((8, heads), F32),
+                ((rows, heads), F32),
+                ((rows, heads), F32),
+                ((rows, 4 * state), F32),
+                ((2 * heads, lanes), BF16),
+            ],
+        )(
+            *(step_raw, bias, decay, step, cum, write_t, read_t, own, within, maps),
+            *(head_inputs, output_grad, returned, *lasts),
+        )
+
+    def grad_half(half, grad):
+        first = half * (steps // 2)
+        in_specs = [head_spec, head_spec, map_spec, line_spec]
+        in_specs += [tokens(lanes, first), tokens(lanes, first)]
+        in_specs += [pl.BlockSpec((here, depth, piece_lanes), lambda i: (first + i, 0, 0))]
+        in_specs += [anywhere] * len(grad)
+        (grad,) = call(
+            functools.partial(grad_kernel, head_width, scale, first * CARRY_HEADS, len(grad)),
+            steps // 2,
+            in_specs,
+            [(tokens(lanes, first), (rows, channels), BF16)],
+            [((rows, heads), F32), ((rows, 2 * state), BF16), ((heads, lanes), BF16)],
+            {len(in_specs) - 1: 0} if half else {},
+        )(step, cum, write_t, skip, output_grad, inner, returned, *grad)
+        return grad
+
+    with jax.named_scope("grad_x"):
+        grad_part = grad_half(0, [table])
+        grad_x = grad_half(1, [grad_part])
 
     with jax.named_scope("projection"):
         tables = [swap(table, "wide", turn) for turn in range(wide)]
         coded = (columns + META, own_model)
         products = pl.pallas_call(
-            functools.partial(product_kernel, planes),
-            in_specs=[pl.BlockSpec(memory_space=pltpu.SMEM)]
-            + [pl.BlockSpec(memory_space=pltpu.VMEM)] * wide
-            + [anywhere] * wide,
+            functools.partial(product_kernel, planes, wide),
+            in_specs=[pl.BlockSpec(memory_space=pltpu.SMEM)] + [anywhere] * (2 * wide + 1),
             out_specs=[pl.BlockSpec(memory_space=pltpu.VMEM)] * planes,
             out_shape=[jax.ShapeDtypeStruct(coded, BF16)] * planes,
             scratch_shapes=[
-                pltpu.VMEM((columns, wide * rows), BF16),
+                pltpu.VMEM((wide, columns, rows), BF16),
                 pltpu.VMEM((planes, wide * rows, own_model), BF16),
-                pltpu.SemaphoreType.DMA((planes, wide)),
+                pltpu.SemaphoreType.DMA((planes + 1, wide)),
             ],
             compiler_params=pltpu.CompilerParams(vmem_limit_bytes=VMEM_LIMIT),
             cost_estimate=SHORT,
-        )(place, *tables, *layer_parts)
+        )(place, *tables, *layer_parts, grad_part)
         sums = [swap(one, "seq", turn) for turn, one in enumerate(products)]
         (weight_grad,) = call(
-            functools.partial(gather_kernel, 1.0 / math.sqrt(rows * blocks)),
+            functools.partial(gather_kernel, 1.0 / math.sqrt(rows * blocks), planes),
             1,
-            [whole(coded)] * planes,
+            [whole(coded)] * planes + [anywhere],
             [(whole((own_model, columns)), (own_model, columns), F32)],
             [],
-        )(*sums)
+        )(*sums, grad_x)
     return grad_x, weight_grad
 
 

time: 196 us -> 193 us (0.985)
  starting transfers between devices: 37.9 us -> 28.8 us
  waiting for transfers between devices: 64.2 us -> 70.5 us
    ppermute x17, waiting for transfers between devices: 62.5 us -> 68.9 us  [swap(): lax.ppermute(array, axis, [(one, one ^ turn) for one in range(count)])]
    all_to_all x3 -> x2, starting transfers between devices: 16.7 us -> 11.9 us  [exchange(): return lax.all_to_all(array, axes, split_axis=0, concat_axis=0, tiled=True)]
    ppermute x17, starting transfers between devices: 21.1 us -> 16.9 us  [swap(): lax.ppermute(array, axis, [(one, one ^ turn) for one in range(count)])]
    pallas_call x9 -> x8, Pallas kernels: 86.3 us -> 85.7 us  [the longest x1 29.4 us: body(): call(functools.partial(block_kernel, head_width, scale, 0, 1), channels /...]
  transfers between devices with their start and end apart: 20 -> 19, of which waited for: 10 -> 8; matrix products, arithmetic and copies ran while one was open for 0% -> 0% of each run, Pallas kernels for 28% -> 25%
where the time goes in v1:
time: 193 us; the launch traced here: 192 us
  Pallas kernels  91.4 us (47%)
  waiting for transfers between devices  70.5 us (37%)
  starting transfers between devices  28.8 us (15%)
    ppermute x17, waiting for transfers between devices, swap(): lax.ppermute(array, axis, [(one, one ^ turn) for one in range(count)])  68.9 us
    pallas_call x1, Pallas kernels, body(): call(functools.partial(block_kernel, head_width, scale, 0, 1), channels /...  29.4 us
    pallas_call x1, Pallas kernels, body(): call(functools.partial(carry_kernel, head_width, scale, len(lasts)), step...  17.8 us
    ppermute x17, starting transfers between devices, swap(): lax.ppermute(array, axis, [(one, one ^ turn) for one in range(count)])  16.9 us
    pallas_call x2, Pallas kernels, grad_half(): call(functools.partial(grad_kernel, head_width, scale, first * CARRY_HEAD...  12.3 us
    all_to_all x2, starting transfers between devices, exchange(): return lax.all_to_all(array, axes, split_axis=0, concat_axis=0, tiled=True)  11.9 us
    pallas_call x1, Pallas kernels, body(): call(functools.partial(summary_kernel, head_width), steps, [head_spec, li...  11 us
    pallas_call x1, Pallas kernels, body(): pl.pallas_call(functools.partial(product_kernel, planes, wide), in_specs=...  6.77 us
  transfers between devices with their start and end apart: 19, of which 8 were waited for; matrix products, arithmetic and copies ran while one was open for 0% of the time, Pallas kernels for 25%

profile of v1, /device:TPU:0, one launch (start us, length us, event | category | flops | bytes accessed | tf_op | source)
XLA Modules:
  0.0 192.1 jit_solution(10077103213810828417)
XLA Ops:
  0.6 11.0 %summaries.1 = (bf16[32,136,256]{2,1,0:T(8,128)(2,1)}, f32[256,128]{1,0:T(8,128)}, f32[256,128]{1,0:T(8,128)}) custom-call(bf16[256,128]{1,0:T(8,128)(2,1)} %refs_0_.1, f32[1,128]{1,0:T(1,128)} %bitcast.17, f32[1,128]{1,0:T(1,128)} %bitcast.19, bf16[64,256]{1,0:T(8,128)(2,1)} %bitcast.7, bf16[64,256]{1,0:T(8,128)(2,1)} %bitcast.12, ...), custom_call_target="tpu_custom_call" | custom-call | flops 1000 | bytes 1000 | tf_op jit(solution)/shard_map/summaries/pallas_call | solution.py:572
  11.6 7.4 %all-to-all-start = ((bf16[32,136,256]{2,1,0:T(8,128)(2,1)}), bf16[32,136,256]{2,1,0:T(8,128)(2,1)}, u32[]{:S(2)}, u32[]{:S(2)}) async-start(bf16[32,136,256]{2,1,0:T(8,128)(2,1)} %get-tuple-element.25), calls=%async_computation | async-start | bytes 4456448 | tf_op jit(solution)/shard_map/scan/all_to_all | solution.py:556
  19.0 0.6 pad_add_fusion.place_ref
  19.6 5.7 %layer.1 = (bf16[4,256,256]{2,1,0:T(8,128)(2,1)}, bf16[4,256,256]{2,1,0:T(8,128)(2,1)}, bf16[4,256,256]{2,1,0:T(8,128)(2,1)}, bf16[4,256,256]{2,1,0:T(8,128)(2,1...) custom-call(s32[2]{0:T(128)} %pad_add_fusion.place_ref, ...), custom_call_target="tpu_custom_call" | custom-call | flops 1000 | bytes 1000 | tf_op jit(solution)/shard_map/layer/pallas_call | solution.py:587
  25.3 0.3 collective-permute-start
  25.6 1.7 collective-permute-start.1
  27.2 1.5 collective-permute-start.2
  28.7 0.0 collective-permute-start.3
  28.7 0.6 collective-permute-start.4
  29.3 29.4 %own_block.1 = (bf16[256,8192]{1,0:T(8,128)(2,1)}, f32[256,128]{1,0:T(8,128)}, f32[256,128]{1,0:T(8,128)}, f32[256,128]{1,0:T(8,128)}) custom-call(f32[256,128]{1,0:T(8,128)} %get-tuple-element.21.step_ref.refs_3_.refs_0_, f32[256,128]{1,0:T(8,128)} %get-tuple-element.22.after_ref.cum_ref.refs_4_.refs_1_, bf16[64,256]{1,0:T(8,128)(2,1)} %bitcast.8, ...), custom_call_target="tpu_custom_call" | custom-call | flops 1000 | bytes 1000 | tf_op jit(solution)/shard_map/own_block/pallas_call | solution.py:609
  58.8 0.0 collective-permute-done.rest_1_.refs_9_
  58.8 0.0 collective-permute-done.1.rest_2_.refs_10_
  58.8 0.0 collective-permute-done.2.rest_3_.refs_12_
  58.8 8.3 %collective-permute-done.3.rest_4_.refs_11_ = bf16[4,256,256]{2,1,0:T(8,128)(2,1)} collective-permute-done((bf16[4,256,256]{2,1,0:T(8,128)(2,1)}, bf16[4,256,256]{2,1,0:T(8,128)(2,1)}, u32[]{:S(2)}, u32[]{:S(2)}) %collective-permute-start.3) | collective-permute-done | bytes 524320 | tf_op jit(solution)/shard_map/layer/ppermute | solution.py:490
  67.1 0.8 collective-permute-done.4.rest_5_.refs_13_
  67.9 1.6 all-to-all-done.message_ref
  69.4 6.2 %scan.1 = bf16[32,136,256]{2,1,0:T(8,128)(2,1)} custom-call(bf16[32,136,256]{2,1,0:T(8,128)(2,1)} %all-to-all-done.message_ref, f32[256,128]{1,0:T(8,128)} %get-tuple-element.26.rest_0_.refs_7_, bf16[4,256,256]{2,1,0:T(8,128)(2,1)} %collective-permute-done.rest_1_.refs_9_, bf16[4,256,256]{2,1,0:T(8,128)(2,1)} %collective-permute-done.1.rest_2_.refs_10_, ...), custom_call_target="tpu_custom_call" | custom-call | flops 1000 | bytes 1000 | tf_op jit(solution)/shard_map/scan/pallas_call | solution.py:630
  75.6 4.5 %all-to-all-start.1 = ((bf16[32,136,256]{2,1,0:T(8,128)(2,1)}), bf16[32,136,256]{2,1,0:T(8,128)(2,1)}, u32[]{:S(2)}, u32[]{:S(2)}) async-start(bf16[32,136,256]{2,1,0:T(8,128)(2,1)} %scan.1), calls=%async_computation.1 | async-start | bytes 4456448 | tf_op jit(solution)/shard_map/scan/all_to_all | solution.py:556
  80.2 2.5 %collective-permute-start.5 = (bf16[4,256,256]{2,1,0:T(8,128)(2,1)S(1)}, bf16[4,256,256]{2,1,0:T(8,128)(2,1)}, u32[]{:S(2)}, u32[]{:S(2)}) collective-permute-start(bf16[4,256,256]{2,1,0:T(8,128)(2,1)S(1)} %copy-done.1), channel_id=1, source_target_pairs={{0,6},{1,7},{2,4},{3,5},{4,2},{5,3},{6,0},{7,1},{8,14},{9,15},{10,... | collective-permute-start | bytes 1572872 | tf_op jit(solution)/shard_map/layer/ppermute | solution.py:490
  82.7 0.0 collective-permute-start.6
  82.7 36.1 %collective-permute-done.5.refs_13_.refs_14_ = bf16[4,256,256]{2,1,0:T(8,128)(2,1)} collective-permute-done((bf16[4,256,256]{2,1,0:T(8,128)(2,1)S(1)}, bf16[4,256,256]{2,1,0:T(8,128)(2,1)}, u32[]{:S(2)}, u32[]{:S(2)}) %collective-permute-start.5) | collective-permute-done | bytes 524320 | tf_op jit(solution)/shard_map/layer/ppermute | solution.py:490
  118.8 15.5 %collective-permute-done.6.refs_14_.refs_15_ = bf16[4,256,256]{2,1,0:T(8,128)(2,1)} collective-permute-done((bf16[4,256,256]{2,1,0:T(8,128)(2,1)S(1)}, bf16[4,256,256]{2,1,0:T(8,128)(2,1)}, u32[]{:S(2)}, u32[]{:S(2)}) %collective-permute-start.6) | collective-permute-done | bytes 524320 | tf_op jit(solution)/shard_map/layer/ppermute | solution.py:490
  134.2 0.0 all-to-all-done.1.refs_12_.refs_6_
  134.2 17.8 %carried.1.refs_7_.refs_0_ = bf16[256,256]{1,0:T(8,128)(2,1)} custom-call(bf16[256,128]{1,0:T(8,128)(2,1)} %refs_0_.1, f32[1,128]{1,0:T(1,128)} %bitcast.18, f32[1,128]{1,0:T(1,128)} %bitcast.20, f32[256,128]{1,0:T(8,128)} %get-tuple-element.21.step_ref.refs_3_.refs_0_, f32[256,128]{1,0:T(8,128)} %get-tuple-element.22.after_ref.cum_ref.refs_4_.refs_1_, ...), custom_call_target="tpu_custom_call" | custom-call | flops 1000 | bytes 1000 | tf_op jit(solution)/shard_map/carried/pallas_call | solution.py:640
  152.1 0.1 collective-permute-start.13
  152.2 2.7 %collective-permute-start.12 = (bf16[256,256]{1,0:T(8,128)(2,1)}, bf16[256,256]{1,0:T(8,128)(2,1)}, u32[]{:S(2)}, u32[]{:S(2)}) collective-permute-start(bf16[256,256]{1,0:T(8,128)(2,1)} %carried.1.refs_7_.refs_0_), channel_id=1, source_target_pairs={{0,6},{1,7},{2,4},{3,5},{4,2},{5,3},{6,0},{7,1},{8,14},{9,15},{10,... | collective-permute-start | bytes 393224 | tf_op jit(solution)/shard_map/projection/ppermute | solution.py:490
  154.9 0.4 collective-permute-start.11
  155.3 1.2 collective-permute-start.10
  156.5 0.7 collective-permute-start.9
  157.2 1.5 collective-permute-done.13.refs_7_
  158.8 0.7 collective-permute-start.8
  159.5 2.8 %collective-permute-done.12.refs_6_ = bf16[256,256]{1,0:T(8,128)(2,1)} collective-permute-done((bf16[256,256]{1,0:T(8,128)(2,1)}, bf16[256,256]{1,0:T(8,128)(2,1)}, u32[]{:S(2)}, u32[]{:S(2)}) %collective-permute-start.12) | collective-permute-done | bytes 131104 | tf_op jit(solution)/shard_map/projection/ppermute | solution.py:490
  162.4 0.0 collective-permute-start.7
  162.4 6.2 %grad_x.2.refs_7_.refs_16_ = bf16[256,8192]{1,0:T(8,128)(2,1)} custom-call(f32[256,128]{1,0:T(8,128)} %get-tuple-element.21.step_ref.refs_3_.refs_0_, f32[256,128]{1,0:T(8,128)} %get-tuple-element.22.after_ref.cum_ref.refs_4_.refs_1_, bf16[64,256]{1,0:T(8,128)(2,1)} %bitcast.10, f32[1,128]{1,0:T(1,128)} %bitcast.15, bf16[256,8192]{1,0:T(8,128)(2,1)} %refs_4_.3, ...), custom_call_target="tpu_custom_call" | custom-call | flops 1000 | bytes 1000 | tf_op jit(solution)/shard_map/grad_x/pallas_call | solution.py:667
  168.5 0.0 collective-permute-done.11.refs_5_
  168.5 0.0 collective-permute-done.10.refs_4_
  168.5 0.0 collective-permute-done.9.refs_3_
  168.5 0.0 collective-permute-done.8.refs_2_
  168.6 0.0 collective-permute-done.7.refs_1_
  168.6 6.8 %projection.2 = (bf16[264,256]{1,0:T(8,128)(2,1)}, bf16[264,256]{1,0:T(8,128)(2,1)}, bf16[264,256]{1,0:T(8,128)(2,1)}, bf16[264,256]{1,0:T(8,128)(2,1)}) custom-call(s32[2]{0:T(128)} %pad_add_fusion.place_ref, bf16[256,256]{1,0:T(8,128)(2,1)} %carried.1.refs_7_.refs_0_, bf16[256,256]{1,0:T(8,128)(2,1)} %collective-permute-done.7.refs_1_, ...), custom_call_target="tpu_custom_call" | custom-call | flops 1000 | bytes 1000 | tf_op jit(solution)/shard_map/projection/pallas_call | solution.py:684
  175.4 1.0 collective-permute-start.14
  176.4 1.7 collective-permute-start.15
  178.1 1.7 collective-permute-start.16
  179.8 6.2 %grad_x.3.refs_4_ = bf16[256,8192]{1,0:T(8,128)(2,1)} custom-call(f32[256,128]{1,0:T(8,128)} %get-tuple-element.21.step_ref.refs_3_.refs_0_, f32[256,128]{1,0:T(8,128)} %get-tuple-element.22.after_ref.cum_ref.refs_4_.refs_1_, bf16[64,256]{1,0:T(8,128)(2,1)} %bitcast.11, f32[1,128]{1,0:T(1,128)} %bitcast.16, ...), custom_call_target="tpu_custom_call", output_to_operand_aliasing={{}: (7, {})} | custom-call | flops 1000 | bytes 1000 | tf_op jit(solution)/shard_map/grad_x/pallas_call | solution.py:667
  186.0 0.0 collective-permute-done.14.refs_1_
  186.0 3.9 %collective-permute-done.15.refs_2_ = bf16[264,256]{1,0:T(8,128)(2,1)} collective-permute-done((bf16[264,256]{1,0:T(8,128)(2,1)}, bf16[264,256]{1,0:T(8,128)(2,1)}, u32[]{:S(2)}, u32[]{:S(2)}) %collective-permute-start.15) | collective-permute-done | bytes 135200 | tf_op jit(solution)/shard_map/projection/ppermute | solution.py:490
  189.9 0.0 collective-permute-done.16.refs_3_
  189.9 2.2 %projection.3 = f32[256,256]{1,0:T(8,128)} custom-call(bf16[264,256]{1,0:T(8,128)(2,1)} %get-tuple-element.36.refs_0_, bf16[264,256]{1,0:T(8,128)(2,1)} %collective-permute-done.14.refs_1_, bf16[264,256]{1,0:T(8,128)(2,1)} %collective-permute-done.15.refs_2_, bf16[264,256]{1,0:T(8,128)(2,1)} %collective-permute-done.16.refs_3_, bf16[256,8192]{1,0:T(8,128)(2,1)} %grad_x.3.refs_4_), custom_call_target="tpu_custom_call" | custom-call | flops 1000 | bytes 1000 | tf_op jit(solution)/shard_map/projection/pallas_call | solution.py:698
  (4 shorter events, 0.0 us)
Async XLA Ops:
  11.6 57.9 %all-to-all-start = ((bf16[32,136,256]{2,1,0:T(8,128)(2,1)}), bf16[32,136,256]{2,1,0:T(8,128)(2,1)}, u32[]{:S(2)}, u32[]{:S(2)}) async-start(bf16[32,136,256]{2,1,0:T(8,128)(2,1)} %get-tuple-element.25), calls=%async_computation | async-start | bytes 4456448 | tf_op jit(solution)/shard_map/scan/all_to_all | solution.py:556
  25.3 33.5 %collective-permute-start = (bf16[4,256,256]{2,1,0:T(8,128)(2,1)}, bf16[4,256,256]{2,1,0:T(8,128)(2,1)}, u32[]{:S(2)}, u32[]{:S(2)}) collective-permute-start(bf16[4,256,256]{2,1,0:T(8,128)(2,1)} %get-tuple-element.27), channel_id=1, source_target_pairs={{0,1},{1,0},{2,3},{3,2},{4,5},{5,4},{6,7},{7,6},{8,9},{9,8},{10,11... | collective-permute-start | bytes 1572872 | tf_op jit(solution)/shard_map/layer/ppermute | solution.py:490
  25.6 33.2 %collective-permute-start.1 = (bf16[4,256,256]{2,1,0:T(8,128)(2,1)}, bf16[4,256,256]{2,1,0:T(8,128)(2,1)}, u32[]{:S(2)}, u32[]{:S(2)}) collective-permute-start(bf16[4,256,256]{2,1,0:T(8,128)(2,1)} %get-tuple-element.28), channel_id=1, source_target_pairs={{0,2},{1,3},{2,0},{3,1},{4,6},{5,7},{6,4},{7,5},{8,10},{9,11},{10,... | collective-permute-start | bytes 1572872 | tf_op jit(solution)/shard_map/layer/ppermute | solution.py:490
  27.2 31.6 %collective-permute-start.2 = (bf16[4,256,256]{2,1,0:T(8,128)(2,1)}, bf16[4,256,256]{2,1,0:T(8,128)(2,1)}, u32[]{:S(2)}, u32[]{:S(2)}) collective-permute-start(bf16[4,256,256]{2,1,0:T(8,128)(2,1)} %get-tuple-element.29), channel_id=1, source_target_pairs={{0,4},{1,5},{2,6},{3,7},{4,0},{5,1},{6,2},{7,3},{8,12},{9,13},{10,... | collective-permute-start | bytes 1572872 | tf_op jit(solution)/shard_map/layer/ppermute | solution.py:490
  28.7 38.4 %collective-permute-start.3 = (bf16[4,256,256]{2,1,0:T(8,128)(2,1)}, bf16[4,256,256]{2,1,0:T(8,128)(2,1)}, u32[]{:S(2)}, u32[]{:S(2)}) collective-permute-start(bf16[4,256,256]{2,1,0:T(8,128)(2,1)} %get-tuple-element.30), channel_id=1, source_target_pairs={{0,3},{1,2},{2,1},{3,0},{4,7},{5,6},{6,5},{7,4},{8,11},{9,10},{10,... | collective-permute-start | bytes 1572872 | tf_op jit(solution)/shard_map/layer/ppermute | solution.py:490
  28.7 39.1 %collective-permute-start.4 = (bf16[4,256,256]{2,1,0:T(8,128)(2,1)}, bf16[4,256,256]{2,1,0:T(8,128)(2,1)}, u32[]{:S(2)}, u32[]{:S(2)}) collective-permute-start(bf16[4,256,256]{2,1,0:T(8,128)(2,1)} %get-tuple-element.31), channel_id=1, source_target_pairs={{0,5},{1,4},{2,7},{3,6},{4,1},{5,0},{6,3},{7,2},{8,13},{9,12},{10,... | collective-permute-start | bytes 1572872 | tf_op jit(solution)/shard_map/layer/ppermute | solution.py:490
  75.6 4.5 %copy-start.1 = (bf16[4,256,256]{2,1,0:T(8,128)(2,1)S(1)}, bf16[4,256,256]{2,1,0:T(8,128)(2,1)}, u32[]{:S(2)}) copy-start(bf16[4,256,256]{2,1,0:T(8,128)(2,1)} %get-tuple-element.34) | copy-start | bytes 1572868
  75.6 7.0 %copy-start = (bf16[4,256,256]{2,1,0:T(8,128)(2,1)S(1)}, bf16[4,256,256]{2,1,0:T(8,128)(2,1)}, u32[]{:S(2)}) copy-start(bf16[4,256,256]{2,1,0:T(8,128)(2,1)} %get-tuple-element.35) | copy-start | bytes 1572868
  75.6 58.6 %all-to-all-start.1 = ((bf16[32,136,256]{2,1,0:T(8,128)(2,1)}), bf16[32,136,256]{2,1,0:T(8,128)(2,1)}, u32[]{:S(2)}, u32[]{:S(2)}) async-start(bf16[32,136,256]{2,1,0:T(8,128)(2,1)} %scan.1), calls=%async_computation.1 | async-start | bytes 4456448 | tf_op jit(solution)/shard_map/scan/all_to_all | solution.py:556
  80.2 38.6 %collective-permute-start.5 = (bf16[4,256,256]{2,1,0:T(8,128)(2,1)S(1)}, bf16[4,256,256]{2,1,0:T(8,128)(2,1)}, u32[]{:S(2)}, u32[]{:S(2)}) collective-permute-start(bf16[4,256,256]{2,1,0:T(8,128)(2,1)S(1)} %copy-done.1), channel_id=1, source_target_pairs={{0,6},{1,7},{2,4},{3,5},{4,2},{5,3},{6,0},{7,1},{8,14},{9,15},{10,... | collective-permute-start | bytes 1572872 | tf_op jit(solution)/shard_map/layer/ppermute | solution.py:490
  82.7 51.6 %collective-permute-start.6 = (bf16[4,256,256]{2,1,0:T(8,128)(2,1)S(1)}, bf16[4,256,256]{2,1,0:T(8,128)(2,1)}, u32[]{:S(2)}, u32[]{:S(2)}) collective-permute-start(bf16[4,256,256]{2,1,0:T(8,128)(2,1)S(1)} %copy-done), channel_id=1, source_target_pairs={{0,7},{1,6},{2,5},{3,4},{4,3},{5,2},{6,1},{7,0},{8,15},{9,14},{10,... | collective-permute-start | bytes 1572872 | tf_op jit(solution)/shard_map/layer/ppermute | solution.py:490
  152.1 6.7 %collective-permute-start.13 = (bf16[256,256]{1,0:T(8,128)(2,1)}, bf16[256,256]{1,0:T(8,128)(2,1)}, u32[]{:S(2)}, u32[]{:S(2)}) collective-permute-start(bf16[256,256]{1,0:T(8,128)(2,1)} %carried.1.refs_7_.refs_0_), channel_id=1, source_target_pairs={{0,7},{1,6},{2,5},{3,4},{4,3},{5,2},{6,1},{7,0},{8,15},{9,14},{10,... | collective-permute-start | bytes 393224 | tf_op jit(solution)/shard_map/projection/ppermute | solution.py:490
  152.2 10.1 %collective-permute-start.12 = (bf16[256,256]{1,0:T(8,128)(2,1)}, bf16[256,256]{1,0:T(8,128)(2,1)}, u32[]{:S(2)}, u32[]{:S(2)}) collective-permute-start(bf16[256,256]{1,0:T(8,128)(2,1)} %carried.1.refs_7_.refs_0_), channel_id=1, source_target_pairs={{0,6},{1,7},{2,4},{3,5},{4,2},{5,3},{6,0},{7,1},{8,14},{9,15},{10,... | collective-permute-start | bytes 393224 | tf_op jit(solution)/shard_map/projection/ppermute | solution.py:490
  154.9 13.6 %collective-permute-start.11 = (bf16[256,256]{1,0:T(8,128)(2,1)}, bf16[256,256]{1,0:T(8,128)(2,1)}, u32[]{:S(2)}, u32[]{:S(2)}) collective-permute-start(bf16[256,256]{1,0:T(8,128)(2,1)} %carried.1.refs_7_.refs_0_), channel_id=1, source_target_pairs={{0,5},{1,4},{2,7},{3,6},{4,1},{5,0},{6,3},{7,2},{8,13},{9,12},{10,... | collective-permute-start | bytes 393224 | tf_op jit(solution)/shard_map/projection/ppermute | solution.py:490
  155.3 13.2 %collective-permute-start.10 = (bf16[256,256]{1,0:T(8,128)(2,1)}, bf16[256,256]{1,0:T(8,128)(2,1)}, u32[]{:S(2)}, u32[]{:S(2)}) collective-permute-start(bf16[256,256]{1,0:T(8,128)(2,1)} %carried.1.refs_7_.refs_0_), channel_id=1, source_target_pairs={{0,4},{1,5},{2,6},{3,7},{4,0},{5,1},{6,2},{7,3},{8,12},{9,13},{10,... | collective-permute-start | bytes 393224 | tf_op jit(solution)/shard_map/projection/ppermute | solution.py:490
  156.5 12.1 %collective-permute-start.9 = (bf16[256,256]{1,0:T(8,128)(2,1)}, bf16[256,256]{1,0:T(8,128)(2,1)}, u32[]{:S(2)}, u32[]{:S(2)}) collective-permute-start(bf16[256,256]{1,0:T(8,128)(2,1)} %carried.1.refs_7_.refs_0_), channel_id=1, source_target_pairs={{0,3},{1,2},{2,1},{3,0},{4,7},{5,6},{6,5},{7,4},{8,11},{9,10},{10,... | collective-permute-start | bytes 393224 | tf_op jit(solution)/shard_map/projection/ppermute | solution.py:490
  158.8 9.8 %collective-permute-start.8 = (bf16[256,256]{1,0:T(8,128)(2,1)}, bf16[256,256]{1,0:T(8,128)(2,1)}, u32[]{:S(2)}, u32[]{:S(2)}) collective-permute-start(bf16[256,256]{1,0:T(8,128)(2,1)} %carried.1.refs_7_.refs_0_), channel_id=1, source_target_pairs={{0,2},{1,3},{2,0},{3,1},{4,6},{5,7},{6,4},{7,5},{8,10},{9,11},{10,... | collective-permute-start | bytes 393224 | tf_op jit(solution)/shard_map/projection/ppermute | solution.py:490
  162.4 6.2 %collective-permute-start.7 = (bf16[256,256]{1,0:T(8,128)(2,1)}, bf16[256,256]{1,0:T(8,128)(2,1)}, u32[]{:S(2)}, u32[]{:S(2)}) collective-permute-start(bf16[256,256]{1,0:T(8,128)(2,1)} %carried.1.refs_7_.refs_0_), channel_id=1, source_target_pairs={{0,1},{1,0},{2,3},{3,2},{4,5},{5,4},{6,7},{7,6},{8,9},{9,8},{10,11... | collective-permute-start | bytes 393224 | tf_op jit(solution)/shard_map/projection/ppermute | solution.py:490
  175.4 10.6 %collective-permute-start.14 = (bf16[264,256]{1,0:T(8,128)(2,1)}, bf16[264,256]{1,0:T(8,128)(2,1)}, u32[]{:S(2)}, u32[]{:S(2)}) collective-permute-start(bf16[264,256]{1,0:T(8,128)(2,1)} %get-tuple-element.37), channel_id=1, source_target_pairs={{0,8},{8,0},{16,24},{24,16},{1,9},{9,1},{17,25},{25,17},{2,10},{10... | collective-permute-start | bytes 405512 | tf_op jit(solution)/shard_map/projection/ppermute | solution.py:490
  176.4 13.5 %collective-permute-start.15 = (bf16[264,256]{1,0:T(8,128)(2,1)}, bf16[264,256]{1,0:T(8,128)(2,1)}, u32[]{:S(2)}, u32[]{:S(2)}) collective-permute-start(bf16[264,256]{1,0:T(8,128)(2,1)} %get-tuple-element.38), channel_id=1, source_target_pairs={{0,16},{8,24},{16,0},{24,8},{1,17},{9,25},{17,1},{25,9},{2,18},{10... | collective-permute-start | bytes 405512 | tf_op jit(solution)/shard_map/projection/ppermute | solution.py:490
  178.1 11.8 %collective-permute-start.16 = (bf16[264,256]{1,0:T(8,128)(2,1)}, bf16[264,256]{1,0:T(8,128)(2,1)}, u32[]{:S(2)}, u32[]{:S(2)}) collective-permute-start(bf16[264,256]{1,0:T(8,128)(2,1)} %get-tuple-element.39), channel_id=1, source_target_pairs={{0,24},{8,16},{16,8},{24,0},{1,25},{9,17},{17,9},{25,1},{2,26},{10... | collective-permute-start | bytes 405512 | tf_op jit(solution)/shard_map/projection/ppermute | solution.py:490
